TPU v7x, 128 devices: a whole 4x4x4 slice. The times are simulated.
128 devices in a mesh: group: 4 (over x), local: 32 (over y, z, core).
Axes of the slice: x: 4, y: 4, z: 4, core: 2. Of those that a mesh axis runs over, the one named last changes fastest.
Arguments:
- tokens: bfloat16 [2048, 3584], P(('group', 'local')), may hold values from -6 to 6
- expert_ids: int32 [2048, 8], P(('group', 'local')), may hold values from 0 to 127, as said below
- gates: float32 [2048, 8], P(('group', 'local')), may hold values from 0.1 to 1
- w_gate: bfloat16 [128, 3584, 1024], P(('group', 'local')), may hold values from -0.09375 to 0.09375
- w_up: bfloat16 [128, 3584, 1024], P(('group', 'local')), may hold values from -0.09375 to 0.09375
- w_down: bfloat16 [128, 1024, 3584], P(('group', 'local')), may hold values from -0.1875 to 0.1875
Outputs:
- mixed: bfloat16 [2048, 3584], P(('group', 'local'))
Inputs may be any that keep to these rules, and one draw needn't show every extreme that they name: `expert_ids`: each token picks 8 different experts, 4 in each of 2 different groups, expert e belonging to group floor(e / 32). Of the 16 tokens of one device at most 2 pick the same expert. One group, the same on all devices, is picked by every token, and each of its experts by exactly 2 tokens of every device.
All inputs are finite; a program needn't handle non-finite values.
Results may differ from a plain program's by a relative error of at most 0.0065.
Values may be sent and summed in bfloat16 or wider, within the bound.
No kernel may reach another device: no remote copies, remote signals or barrier semaphores. Data moves between devices by JAX's collectives and lax.ppermute only.
A program may use at most 128 MiB of HBM per device.

v0:
```python
import jax
import jax.numpy as jnp
from jax import lax
from jax.sharding import PartitionSpec as P

GROUPS_USED = 2


def expert_ffn(slab_rows, gate_matrix, up_matrix, down_matrix):
    flat_rows = slab_rows.reshape(-1, slab_rows.shape[-1])
    gate_part = jnp.dot(flat_rows, gate_matrix, preferred_element_type=jnp.float32)
    up_part = jnp.dot(flat_rows, up_matrix, preferred_element_type=jnp.float32)
    hidden = (jax.nn.silu(gate_part) * up_part).astype(jnp.bfloat16)
    produced = jnp.dot(hidden, down_matrix, preferred_element_type=jnp.float32).astype(jnp.bfloat16)
    return produced.reshape(slab_rows.shape)


def pick_ranks(labels, label_count):
    onehot = (labels[:, None] == jnp.arange(label_count, dtype=jnp.int32)[None, :]).astype(
        jnp.int32
    )
    return jnp.sum(jnp.cumsum(onehot, axis=0) * onehot, axis=1) - 1


def weighted_sum(weights, picked):
    return jnp.sum(weights[:, :, None] * picked.astype(jnp.float32), axis=1)


def on_device(tokens, expert_ids, gates, w_gate, w_up, w_down):
    group_count = lax.axis_size("group")
    local_count = lax.axis_size("local")
    expert_count = group_count * local_count
    tok_count, model_width = tokens.shape
    top_count = expert_ids.shape[1]
    per_group = top_count // GROUPS_USED
    capacity = per_group * tok_count // local_count
    gate_matrix = w_gate[0]
    up_matrix = w_up[0]
    down_matrix = w_down[0]
    zero_row = jnp.zeros((1, model_width), jnp.bfloat16)
    group_of = expert_ids // local_count
    flat_ids = expert_ids.reshape(-1)
    slot_rank = pick_ranks(flat_ids, expert_count)
    target = flat_ids * capacity + slot_rank
    owner = jnp.arange(flat_ids.shape[0], dtype=jnp.int32) // top_count
    slot_source = jnp.full((expert_count * capacity,), tok_count, jnp.int32).at[target].set(owner)
    padded_tokens = jnp.concatenate([tokens, zero_row], axis=0)
    outgoing = padded_tokens[slot_source].reshape(expert_count, capacity, model_width)
    produced = expert_ffn(
        lax.all_to_all(outgoing, ("group", "local"), split_axis=0, concat_axis=0, tiled=True),
        gate_matrix,
        up_matrix,
        down_matrix,
    )
    returned = lax.all_to_all(produced, ("group", "local"), split_axis=0, concat_axis=0, tiled=True)
    picked = returned.reshape(-1, model_width)[target].reshape(tok_count, top_count, model_width)
    total = jnp.zeros((tok_count, model_width), jnp.float32)
    for group_index in range(group_count):
        weights = jnp.where(group_of == group_index, gates, jnp.zeros_like(gates))
        partial_sum = lax.optimization_barrier(weighted_sum(weights, picked).astype(jnp.bfloat16))
        total = total + partial_sum.astype(jnp.float32)
    return total.astype(jnp.bfloat16)


def solution(mesh):
    placed = (
        P(("group", "local"), None),
        P(("group", "local"), None),
        P(("group", "local"), None),
        P(("group", "local"), None, None),
        P(("group", "local"), None, None),
        P(("group", "local"), None, None),
    )
    return jax.shard_map(
        on_device,
        mesh=mesh,
        in_specs=placed,
        out_specs=P(("group", "local"), None),
        check_vma=False,
    )
```

profile of v0, /device:TPU:1, one launch (start us, length us, event | category | flops | bytes accessed | tf_op | source)
XLA Modules:
  0.0 111.7 jit_solution(7622952835933568411)
XLA Ops:
  0.0 0.8 copy.15
  0.8 0.7 broadcast_multiply_fusion
  1.5 0.1 eq.34
  1.5 0.1 fusion.22
  1.6 0.2 reduce_window_sum.11
  1.8 0.2 select_reduce_fusion
  2.0 0.1 copy.14
  2.1 0.1 mul.61
  2.2 1.0 scatter_custom_fusion
  3.2 0.9 concatenate.3
  4.1 1.7 %gather_fusion = bf16[256,3584]{1,0:T(8,128)(2,1)S(1)} fusion(bf16[17,3584]{1,0:T(8,128)(2,1)S(1)} %concatenate.3, s32[1024]{0:T(1024)S(1)} %pad_clamp_fusion.1), kind=kCustom, calls=%fused_computation | custom fusion | bytes 3671040 | tf_op jit(solution)/shard_map/gather | solution.py:48
  5.8 1.7 %reshape.54 = bf16[128,2,3584]{2,1,0:T(2,128)(2,1)} reshape(bf16[256,3584]{1,0:T(8,128)(2,1)S(1)} %gather_fusion) | data formatting | bytes 3670016 | tf_op jit(solution)/shard_map/reshape | solution.py:48
  7.5 39.2 %all_to_all.10 = bf16[128,2,3584]{2,1,0:T(2,128)(2,1)S(1)} all-to-all(bf16[128,2,3584]{2,1,0:T(2,128)(2,1)} %reshape.54), channel_id=1, replica_groups=mesh['group'=4,'local'=32] {'group','local'}, dimensions={0} | all-to-all | bytes 3670016 | tf_op jit(solution)/shard_map/all_to_all | solution.py:50
  46.7 1.7 %reshape.55 = bf16[256,3584]{1,0:T(8,128)(2,1)} reshape(bf16[128,2,3584]{2,1,0:T(2,128)(2,1)S(1)} %all_to_all.10) | data formatting | bytes 3670016 | tf_op jit(solution)/shard_map/reshape | solution.py:10
  48.4 5.8 %fusion.4 = f32[256,1024]{1,0:T(8,128)S(1)} fusion(bf16[256,3584]{1,0:T(8,128)(2,1)} %reshape.55, bf16[1,3584,1024]{2,1,0:T(8,128)(2,1)} %param.9), kind=kOutput, calls=%fused_computation.7 | convolution fusion | flops 1879048192 | bytes 10223616 | tf_op jit(solution)/shard_map/dot_general | solution.py:11
  54.2 10.6 %fusion.6 = bf16[256,3584]{1,0:T(8,128)(2,1)} fusion(bf16[1,1024,3584]{2,1,0:T(8,128)(2,1)} %param.11, bf16[256,3584]{1,0:T(8,128)(2,1)S(1)} %copy-done, bf16[1,3584,1024]{2,1,0:T(8,128)(2,1)} %param.10, f32[256,1024]{1,0:T(8,128)S(1)} %fusion.4), kind=kOutput, calls=%fused_computation.9 | convolution fusion | flops 3760586752 | bytes 19398656 | tf_op jit(solution)/shard_map/dot_general | solution.py:14
  64.8 4.8 %reshape.56 = bf16[128,2,3584]{2,1,0:T(2,128)(2,1)} reshape(bf16[256,3584]{1,0:T(8,128)(2,1)} %fusion.6) | data formatting | bytes 3670016 | tf_op jit(solution)/shard_map/reshape | solution.py:15
  69.6 5.8 %all-to-all-start.1 = ((bf16[128,2,3584]{2,1,0:T(2,128)(2,1)}), bf16[128,2,3584]{2,1,0:T(2,128)(2,1)}, u32[]{:S(2)}, u32[]{:S(2)}) async-start(bf16[128,2,3584]{2,1,0:T(2,128)(2,1)} %reshape.56), calls=%async_computation.1 | async-start | bytes 3670016 | tf_op jit(solution)/shard_map/all_to_all | solution.py:55
  75.4 0.1 copy.13
  75.7 27.2 %all-to-all-done.1 = bf16[128,2,3584]{2,1,0:T(2,128)(2,1)} async-done(((bf16[128,2,3584]{2,1,0:T(2,128)(2,1)}), bf16[128,2,3584]{2,1,0:T(2,128)(2,1)}, u32[]{:S(2)}, u32[]{:S(2)}) %all-to-all-start.1) | async-done | bytes 1835040 | tf_op jit(solution)/shard_map/all_to_all | solution.py:55
  102.9 4.1 %reshape.57 = bf16[256,3584]{1,0:T(8,128)(2,1)S(1)} reshape(bf16[128,2,3584]{2,1,0:T(2,128)(2,1)} %all-to-all-done.1) | data formatting | bytes 3670016 | tf_op jit(solution)/shard_map/reshape | solution.py:56
  107.0 1.1 gather_fusion.1
  108.1 2.9 %fusion.9 = (bf16[16,3584]{1,0:T(8,128)(2,1)S(1)}, bf16[16,3584]{1,0:T(8,128)(2,1)S(1)}, bf16[16,3584]{1,0:T(8,128)(2,1)S(1)}, bf16[16,3584]{1,0:T(8,128)(2,1)S(1)}) fusion(bf16[128,3584]{1,0:T(8,128)(2,1)S(1)} %gather_fusion.1, f32[16,8]{1,0:T(8,128)S(1)} %copy.13, f32[16,8]{1,0:T(8,128)S(1)} %copy.18, f32[16,8]{1,0:T(8,128)S(1)} %copy.17, f32[16,8]{1,0:T(8,128)S(1)} %copy.16), kind=kLoop, calls=%fused_computation.14 | loop fusion | flops 3899392 | bytes 1378304 | tf_op jit(solution)/shard_map/reduce_sum | solution.py:26
  111.0 0.7 add_convert_fusion
  (15 shorter events, 0.3 us)
Async XLA Ops:
  48.4 5.8 %copy-start = (bf16[256,3584]{1,0:T(8,128)(2,1)S(1)}, bf16[256,3584]{1,0:T(8,128)(2,1)}, u32[]{:S(2)}) copy-start(bf16[256,3584]{1,0:T(8,128)(2,1)} %reshape.55) | copy-start | bytes 5505028
  69.6 5.8 %copy-start.1 = (s32[16,8]{0,1:T(8,128)S(1)}, s32[16,8]{0,1:T(8,128)}, u32[]{:S(2)}) copy-start(s32[16,8]{0,1:T(8,128)} %param.7) | copy-start | bytes 1540
  69.6 5.8 %copy-start.2 = (f32[16,8]{0,1:T(8,128)S(1)}, f32[16,8]{0,1:T(8,128)}, u32[]{:S(2)}) copy-start(f32[16,8]{0,1:T(8,128)} %param.8) | copy-start | bytes 1540
  69.6 33.3 %all-to-all-start.1 = ((bf16[128,2,3584]{2,1,0:T(2,128)(2,1)}), bf16[128,2,3584]{2,1,0:T(2,128)(2,1)}, u32[]{:S(2)}, u32[]{:S(2)}) async-start(bf16[128,2,3584]{2,1,0:T(2,128)(2,1)} %reshape.56), calls=%async_computation.1 | async-start | bytes 3670016 | tf_op jit(solution)/shard_map/all_to_all | solution.py:55
where the time goes:
time: 112 us
  blocking collectives  39.2 us (35%)
  waiting for transfers between devices  27.2 us (24%)
  local copies, waits for them, and re-layouts  18.2 us (16%)
  matrix products  16.4 us (15%)
  starting transfers between devices  5.76 us (5%)
  other arithmetic  4.76 us (4%)
    all_to_all x1, blocking collectives, on_device(): lax.all_to_all(outgoing, ('group', 'local'), split_axis=0, concat_axis=0,...  39.2 us
    all_to_all x1, waiting for transfers between devices, on_device(): lax.all_to_all(produced, ('group', 'local'), split_axis=0, concat_axis=0,...  27.2 us
    dot_general x1, matrix products, expert_ffn(): jnp.dot(hidden, down_matrix, preferred_element_type=jnp.float32)  10.6 us
    dot_general x1, matrix products, expert_ffn(): jnp.dot(flat_rows, gate_matrix, preferred_element_type=jnp.float32)  5.82 us
    all_to_all x1, starting transfers between devices, on_device(): lax.all_to_all(produced, ('group', 'local'), split_axis=0, concat_axis=0,...  5.76 us
    reshape x1, local copies, waits for them, and re-layouts, expert_ffn(): return produced.reshape(slab_rows.shape)  4.79 us
    reshape x1, local copies, waits for them, and re-layouts, on_device(): returned.reshape(-1, model_width)[target]  4.06 us
    reduce_sum x1, other arithmetic, weighted_sum(): return jnp.sum(weights[:, :, None] * picked.astype(jnp.float32), axis=1)  2.9 us
  transfers between devices with their start and end apart: 1, of which 1 were waited for; matrix products, arithmetic and copies ran while one was open for 0% of the time, Pallas kernels for 0%

commit v1 on v0

v1 whole, which is shorter than its diff:
```python
import functools

import jax
import jax.numpy as jnp
from jax import lax
from jax.experimental import pallas as pl
from jax.experimental.pallas import tpu as pltpu
from jax.sharding import PartitionSpec as P

CAPACITY = 2
QUARTERS = 4
PART = CAPACITY * QUARTERS
LANES = 128
VMEM = pl.BlockSpec(memory_space=pltpu.VMEM)


def pack_kernel(ids_ref, tokens_ref, out_ref, cut):
    top, tok = ids_ref.shape
    rows = out_ref.shape[0]
    tiles = out_ref.shape[1] // LANES
    wide = QUARTERS * tok
    for q in range(QUARTERS):
        for j in range(tiles):
            column = (j * QUARTERS + q) * LANES
            cut[q * tok:(q + 1) * tok, j * LANES:(j + 1) * LANES] = tokens_ref[:, column:column + LANES]
    t_of = lax.broadcasted_iota(jnp.int32, (tok, wide), 0)
    c_of = lax.broadcasted_iota(jnp.int32, (tok, wide), 1)
    spread = (lax.rem(c_of, tok) == t_of).astype(jnp.float32)
    ids = jnp.dot(ids_ref[...].astype(jnp.float32), spread, preferred_element_type=jnp.float32).astype(jnp.int32)
    row = lax.broadcasted_iota(jnp.int32, (rows, wide), 0)
    column = lax.broadcasted_iota(jnp.int32, (rows, wide), 1)
    expert = row // PART
    picked = expert == ids[0:1, :]
    for k in range(1, top):
        picked = picked | (expert == ids[k:k + 1, :])
    a = lax.broadcasted_iota(jnp.int32, (wide, wide), 0)
    b = lax.broadcasted_iota(jnp.int32, (wide, wide), 1)
    before = ((a // tok == b // tok) & (a < b)).astype(jnp.bfloat16)
    rank = jnp.dot(picked.astype(jnp.bfloat16), before, preferred_element_type=jnp.float32)
    slot = lax.rem(row, CAPACITY)
    quarter = lax.rem(row // CAPACITY, QUARTERS)
    chosen = picked & (rank == slot.astype(jnp.float32)) & (quarter == column // tok)
    out_ref[...] = jnp.dot(
        chosen.astype(jnp.bfloat16), cut[...], preferred_element_type=jnp.float32
    ).astype(jnp.bfloat16)


def pack(ids, tokens, experts):
    tok, width = tokens.shape
    return pl.pallas_call(
        pack_kernel,
        out_shape=jax.ShapeDtypeStruct((experts * PART, width // QUARTERS), jnp.bfloat16),
        in_specs=[VMEM, VMEM],
        out_specs=VMEM,
        scratch_shapes=[pltpu.VMEM((QUARTERS * tok, width // QUARTERS), jnp.bfloat16)],
        compiler_params=pltpu.CompilerParams(vmem_limit_bytes=16 << 20),
    )(ids, tokens)


def weigh_kernel(ids_ref, gates_ref, out_ref):
    top, tok = ids_ref.shape
    rows = out_ref.shape[1]
    wide = QUARTERS * tok
    w_of = lax.broadcasted_iota(jnp.int32, (wide, tok), 0)
    t_of = lax.broadcasted_iota(jnp.int32, (wide, tok), 1)
    spread = (lax.rem(w_of, tok) == t_of).astype(jnp.float32)
    contract = (((1,), (1,)), ((), ()))
    ids = lax.dot_general(
        spread, ids_ref[...].astype(jnp.float32), contract, preferred_element_type=jnp.float32
    ).astype(jnp.int32)
    gates = lax.dot_general(
        spread, gates_ref[...], contract,
        precision=lax.Precision.HIGHEST, preferred_element_type=jnp.float32,
    )
    line = lax.broadcasted_iota(jnp.int32, (wide, rows), 0)
    row = lax.broadcasted_iota(jnp.int32, (wide, rows), 1)
    expert = row // PART
    weight = jnp.zeros((wide, rows), jnp.float32)
    picked = jnp.zeros((wide, rows), jnp.float32)
    for k in range(top):
        hit = expert == ids[:, k:k + 1]
        weight = jnp.where(hit, gates[:, k:k + 1], weight)
        picked = jnp.where(hit, 1.0, picked)
    a = lax.broadcasted_iota(jnp.int32, (wide, wide), 0)
    b = lax.broadcasted_iota(jnp.int32, (wide, wide), 1)
    before = ((a // tok == b // tok) & (b < a)).astype(jnp.bfloat16)
    rank = jnp.dot(before, picked.astype(jnp.bfloat16), preferred_element_type=jnp.float32)
    slot = lax.rem(row, CAPACITY)
    quarter = lax.rem(row // CAPACITY, QUARTERS)
    weight = jnp.where((rank == slot.astype(jnp.float32)) & (quarter == line // tok), weight, 0.0)
    high = weight.astype(jnp.bfloat16)
    out_ref[0:wide, :] = high
    out_ref[wide:2 * wide, :] = (weight - high.astype(jnp.float32)).astype(jnp.bfloat16)


def weigh(ids, gates, experts):
    tok = ids.shape[1]
    return pl.pallas_call(
        weigh_kernel,
        out_shape=jax.ShapeDtypeStruct((2 * QUARTERS * tok, experts * PART), jnp.bfloat16),
        in_specs=[VMEM, VMEM],
        out_specs=VMEM,
        compiler_params=pltpu.CompilerParams(vmem_limit_bytes=16 << 20),
    )(ids, gates)


def combine_kernel(weights_ref, returned_ref, out_ref):
    tok = out_ref.shape[0]
    wide = QUARTERS * tok
    tiles = returned_ref.shape[1] // LANES
    both = jnp.dot(weights_ref[...], returned_ref[...], preferred_element_type=jnp.float32)
    total = (both[0:wide] + both[wide:2 * wide]).astype(jnp.bfloat16)
    for q in range(QUARTERS):
        for j in range(tiles):
            column = (j * QUARTERS + q) * LANES
            out_ref[:, column:column + LANES] = total[q * tok:(q + 1) * tok, j * LANES:(j + 1) * LANES]


def combine(weights, returned, tok):
    width = returned.shape[1] * QUARTERS
    return pl.pallas_call(
        combine_kernel,
        out_shape=jax.ShapeDtypeStruct((tok, width), jnp.bfloat16),
        in_specs=[VMEM, VMEM],
        out_specs=VMEM,
        compiler_params=pltpu.CompilerParams(vmem_limit_bytes=16 << 20),
    )(weights, returned)


def expert_kernel(
    got_ref, gate_hbm, up_hbm, down_hbm, out_ref,
    gate_buf, up_buf, down_buf, wide_buf, rows_buf, hidden_buf, gate_sem, up_sem, down_sem,
):
    ff_steps, _, ff_tile = gate_buf.shape
    d_steps, _, d_tile = down_buf.shape
    rows = got_ref.shape[0]
    sources = rows // PART

    def gate_copy(f):
        return pltpu.make_async_copy(gate_hbm.at[:, pl.ds(f * ff_tile, ff_tile)], gate_buf.at[f], gate_sem.at[f])

    def up_copy(f):
        return pltpu.make_async_copy(up_hbm.at[:, pl.ds(f * ff_tile, ff_tile)], up_buf.at[f], up_sem.at[f])

    def down_copy(n):
        return pltpu.make_async_copy(down_hbm.at[:, pl.ds(n * d_tile, d_tile)], down_buf.at[n], down_sem.at[n])

    for f in range(ff_steps):
        gate_copy(f).start()
        up_copy(f).start()
    for n in range(d_steps):
        down_copy(n).start()

    for j in range(d_steps):
        wide_buf[j] = got_ref[:, j * LANES:(j + 1) * LANES].astype(jnp.float32)
    for slot in range(CAPACITY):
        for q in range(QUARTERS):
            for j in range(d_steps):
                piece = wide_buf[j, pl.ds(q * CAPACITY + slot, sources, stride=PART), :]
                column = (j * QUARTERS + q) * LANES
                rows_buf[slot * sources:(slot + 1) * sources, column:column + LANES] = piece.astype(jnp.bfloat16)

    for f in range(ff_steps):
        gate_copy(f).wait()
        gate_part = jnp.dot(rows_buf[...], gate_buf[f], preferred_element_type=jnp.float32)
        up_copy(f).wait()
        up_part = jnp.dot(rows_buf[...], up_buf[f], preferred_element_type=jnp.float32)
        hidden = gate_part / (1.0 + jnp.exp(-gate_part)) * up_part
        hidden_buf[:, f * ff_tile:(f + 1) * ff_tile] = hidden.astype(jnp.bfloat16)

    for n in range(d_steps):
        down_copy(n).wait()
        produced = jnp.dot(hidden_buf[...], down_buf[n], preferred_element_type=jnp.float32)
        for slot in range(CAPACITY):
            for q in range(QUARTERS):
                wide_buf[n, pl.ds(q * CAPACITY + slot, sources, stride=PART), :] = produced[
                    slot * sources:(slot + 1) * sources, q * LANES:(q + 1) * LANES
                ]
        out_ref[:, n * LANES:(n + 1) * LANES] = wide_buf[n].astype(jnp.bfloat16)


def expert_ffn(got, gate_matrix, up_matrix, down_matrix):
    rows, _ = got.shape
    width, ff = gate_matrix.shape
    ff_tile = 256
    d_tile = QUARTERS * LANES
    ff_steps, d_steps = ff // ff_tile, width // d_tile
    any_spec = pl.BlockSpec(memory_space=pl.ANY)
    return pl.pallas_call(
        expert_kernel,
        out_shape=jax.ShapeDtypeStruct(got.shape, jnp.bfloat16),
        in_specs=[VMEM, any_spec, any_spec, any_spec],
        out_specs=VMEM,
        scratch_shapes=[
            pltpu.VMEM((ff_steps, width, ff_tile), jnp.bfloat16),
            pltpu.VMEM((ff_steps, width, ff_tile), jnp.bfloat16),
            pltpu.VMEM((d_steps, ff, d_tile), jnp.bfloat16),
            pltpu.VMEM((d_steps, rows, LANES), jnp.float32),
            pltpu.VMEM((rows // QUARTERS, width), jnp.bfloat16),
            pltpu.VMEM((rows // QUARTERS, ff), jnp.bfloat16),
            pltpu.SemaphoreType.DMA((ff_steps,)),
            pltpu.SemaphoreType.DMA((ff_steps,)),
            pltpu.SemaphoreType.DMA((d_steps,)),
        ],
        compiler_params=pltpu.CompilerParams(vmem_limit_bytes=48 << 20),
    )(got, gate_matrix, up_matrix, down_matrix)


def swap(messages, experts):
    parts = messages.reshape(experts, PART, messages.shape[1])
    moved = lax.all_to_all(parts, ("group", "local"), split_axis=0, concat_axis=0, tiled=True)
    return moved.reshape(messages.shape)


def on_device(tokens, expert_ids, gates, w_gate, w_up, w_down):
    experts = lax.axis_size("group") * lax.axis_size("local")
    ids = expert_ids.T
    got = swap(pack(ids, tokens, experts), experts)
    produced = expert_ffn(got, w_gate[0], w_up[0], w_down[0])
    weights = weigh(ids, gates.T, experts)
    returned = swap(produced, experts)
    return combine(weights, returned, tokens.shape[0])


def solution(mesh):
    placed = (
        P(("group", "local"), None),
        P(("group", "local"), None),
        P(("group", "local"), None),
        P(("group", "local"), None, None),
        P(("group", "local"), None, None),
        P(("group", "local"), None, None),
    )
    return jax.shard_map(
        on_device,
        mesh=mesh,
        in_specs=placed,
        out_specs=P(("group", "local"), None),
        check_vma=False,
    )
```

time: 112 us -> 91.8 us (0.82)
  Pallas kernels: 0 us -> 19 us
  local copies, waits for them, and re-layouts: 18.2 us -> 1.6 us
  matrix products: 16.4 us -> 0 us
  other arithmetic: 4.76 us -> 0 us
  starting transfers between devices: 5.76 us -> 4.63 us
    pallas_call x0 -> x4, Pallas kernels: none -> 19 us  [the longest x1 16.1 us: expert_ffn(): pl.pallas_call(expert_kernel, out_shape=jax.ShapeDtypeStruct(got.shape, j...]
    dot_general x2 -> x0, matrix products: 16.4 us -> none  [the longest x1 10.6 us: expert_ffn(): jnp.dot(hidden, down_matrix, preferred_element_type=jnp.float32)]
    reshape x4 -> x0, local copies, waits for them, and re-layouts: 12.2 us -> none  [the longest x1 4.79 us: expert_ffn(): return produced.reshape(slab_rows.shape)]
    reduce_sum x2 -> x0, other arithmetic: 3.07 us -> none  [the longest x1 2.9 us: weighted_sum(): return jnp.sum(weights[:, :, None] * picked.astype(jnp.float32), axis=1)]
    gather x2 -> x0, local copies, waits for them, and re-layouts: 2.83 us -> none  [the longest x1 1.72 us: on_device(): padded_tokens[slot_source].reshape(expert_count, capacity, model_width)]
    all_to_all x1, starting transfers between devices: 5.76 us -> 4.63 us  [swap(): lax.all_to_all(parts, ('group', 'local'), split_axis=0, concat_axis=0, ti...]
  transfers between devices with their start and end apart: 1 -> 1, of which waited for: 1 -> 1; matrix products, arithmetic and copies ran while one was open for 0% -> 0% of each run, Pallas kernels for 0% -> 1%
where the time goes in v1:
time: 91.8 us; the launch traced here: 91.5 us
  blocking collectives  39 us (42%)
  waiting for transfers between devices  27.3 us (30%)
  Pallas kernels  19 us (21%)
  starting transfers between devices  4.63 us (5%)
  local copies, waits for them, and re-layouts  1.6 us (2%)
    all_to_all x1, blocking collectives, swap(): lax.all_to_all(parts, ('group', 'local'), split_axis=0, concat_axis=0, ti...  39 us
    all_to_all x1, waiting for transfers between devices, swap(): lax.all_to_all(parts, ('group', 'local'), split_axis=0, concat_axis=0, ti...  27.3 us
    pallas_call x1, Pallas kernels, expert_ffn(): pl.pallas_call(expert_kernel, out_shape=jax.ShapeDtypeStruct(got.shape, j...  16.1 us
    all_to_all x1, starting transfers between devices, swap(): lax.all_to_all(parts, ('group', 'local'), split_axis=0, concat_axis=0, ti...  4.63 us
  transfers between devices with their start and end apart: 1, of which 1 were waited for; matrix products, arithmetic and copies ran while one was open for 0% of the time, Pallas kernels for 1%

profile of v1, /device:TPU:1, one launch (start us, length us, event | category | flops | bytes accessed | tf_op | source)
XLA Modules:
  0.0 91.5 jit_solution(5703427736593591357)
XLA Ops:
  0.0 0.0 copy-start
  0.0 0.9 copy-done
  0.9 0.0 copy-start.1
  0.9 0.7 copy-done.1
  1.6 1.2 %shard_map.65 = bf16[1024,896]{1,0:T(8,128)(2,1)S(1)} custom-call(s32[8,16]{1,0:T(8,128)S(1)} %bitcast.12, bf16[16,3584]{1,0:T(8,128)(2,1)S(1)} %copy-done), custom_call_target="tpu_custom_call" | custom-call | tf_op jit(solution)/shard_map/pallas_call | solution.py:50
  2.8 39.0 %all_to_all.10 = bf16[128,8,896]{2,1,0:T(8,128)(2,1)S(1)} all-to-all(bf16[128,8,896]{2,1,0:T(8,128)(2,1)S(1)} %bitcast.11), channel_id=1, replica_groups=mesh['group'=4,'local'=32] {'group','local'}, dimensions={0} | all-to-all | bytes 3670016 | tf_op jit(solution)/shard_map/all_to_all | solution.py:211
  41.8 16.1 %shard_map.66 = bf16[1024,896]{1,0:T(8,128)(2,1)} custom-call(bf16[1024,896]{1,0:T(8,128)(2,1)S(1)} %bitcast.9, bf16[3584,1024]{1,0:T(8,128)(2,1)} %bitcast.15, bf16[3584,1024]{1,0:T(8,128)(2,1)} %bitcast.16, bf16[1024,3584]{1,0:T(8,128)(2,1)} %bitcast.17), custom_call_target="tpu_custom_call" | custom-call | tf_op jit(solution)/shard_map/pallas_call | solution.py:189
  57.9 0.0 copy-start.2
  58.0 0.0 copy-start.3
  58.0 4.6 %all-to-all-start.1 = ((bf16[128,8,896]{2,1,0:T(8,128)(2,1)}), bf16[128,8,896]{2,1,0:T(8,128)(2,1)S(1)}, u32[]{:S(2)}, u32[]{:S(2)}) async-start(bf16[128,8,896]{2,1,0:T(8,128)(2,1)} %bitcast.7), calls=%async_computation.1 | async-start | bytes 3670016 | tf_op jit(solution)/shard_map/all_to_all | solution.py:211
  62.6 0.0 copy-done.2
  62.6 0.0 copy-done.3
  62.6 0.6 shard_map.64.weights_ref
  63.2 27.3 %all-to-all-done.1 = bf16[128,8,896]{2,1,0:T(8,128)(2,1)S(1)} async-done(((bf16[128,8,896]{2,1,0:T(8,128)(2,1)}), bf16[128,8,896]{2,1,0:T(8,128)(2,1)S(1)}, u32[]{:S(2)}, u32[]{:S(2)}) %all-to-all-start.1) | async-done | bytes 1835040 | tf_op jit(solution)/shard_map/all_to_all | solution.py:211
  90.4 1.1 %shard_map.67 = bf16[16,3584]{1,0:T(8,128)(2,1)} custom-call(bf16[128,1024]{1,0:T(8,128)(2,1)S(1)} %shard_map.64.weights_ref, bf16[1024,896]{1,0:T(8,128)(2,1)S(1)} %bitcast.10), custom_call_target="tpu_custom_call" | custom-call | tf_op jit(solution)/shard_map/pallas_call | solution.py:121
Async XLA Ops:
  0.0 0.9 copy-start
  0.9 0.7 copy-start.1
  57.9 4.7 %copy-start.2 = (s32[16,8]{0,1:T(8,128)S(1)}, s32[16,8]{0,1:T(8,128)}, u32[]{:S(2)}) copy-start(s32[16,8]{0,1:T(8,128)} %param.7) | copy-start | bytes 1540
  58.0 4.7 %copy-start.3 = (f32[16,8]{0,1:T(8,128)S(1)}, f32[16,8]{0,1:T(8,128)}, u32[]{:S(2)}) copy-start(f32[16,8]{0,1:T(8,128)} %param.8) | copy-start | bytes 1540
  58.0 32.5 %all-to-all-start.1 = ((bf16[128,8,896]{2,1,0:T(8,128)(2,1)}), bf16[128,8,896]{2,1,0:T(8,128)(2,1)S(1)}, u32[]{:S(2)}, u32[]{:S(2)}) async-start(bf16[128,8,896]{2,1,0:T(8,128)(2,1)} %bitcast.7), calls=%async_computation.1 | async-start | bytes 3670016 | tf_op jit(solution)/shard_map/all_to_all | solution.py:211

commit v2 on v1

v2 whole, which is shorter than its diff:
```python
import jax
import jax.numpy as jnp
from jax import lax
from jax.experimental import pallas as pl
from jax.experimental.pallas import tpu as pltpu
from jax.sharding import PartitionSpec as P

CAPACITY = 2
QUARTERS = 4
PART = CAPACITY * QUARTERS
LANES = 128
FF_TILE = 256
AHEAD = 3
DOWN_PARTS = 3
VMEM = pl.BlockSpec(memory_space=pltpu.VMEM)
ANYWHERE = pl.BlockSpec(memory_space=pl.ANY)


def pack_kernel(ids_hbm, tokens_hbm, out_ref, ids_ref, tokens_ref, cut, sems):
    ids_copy = pltpu.make_async_copy(ids_hbm, ids_ref, sems.at[0])
    tokens_copy = pltpu.make_async_copy(tokens_hbm, tokens_ref, sems.at[1])
    ids_copy.start()
    tokens_copy.start()
    top, tok = ids_ref.shape
    rows = out_ref.shape[0]
    tiles = out_ref.shape[1] // LANES
    wide = QUARTERS * tok
    t_of = lax.broadcasted_iota(jnp.int32, (tok, wide), 0)
    c_of = lax.broadcasted_iota(jnp.int32, (tok, wide), 1)
    spread = (lax.rem(c_of, tok) == t_of).astype(jnp.float32)
    ids_copy.wait()
    ids = jnp.dot(ids_ref[...].astype(jnp.float32), spread, preferred_element_type=jnp.float32).astype(jnp.int32)
    row = lax.broadcasted_iota(jnp.int32, (rows, wide), 0)
    column = lax.broadcasted_iota(jnp.int32, (rows, wide), 1)
    expert = row // PART
    picked = expert == ids[0:1, :]
    for k in range(1, top):
        picked = picked | (expert == ids[k:k + 1, :])
    a = lax.broadcasted_iota(jnp.int32, (wide, wide), 0)
    b = lax.broadcasted_iota(jnp.int32, (wide, wide), 1)
    before = ((a // tok == b // tok) & (a < b)).astype(jnp.bfloat16)
    rank = jnp.dot(picked.astype(jnp.bfloat16), before, preferred_element_type=jnp.float32)
    slot = lax.rem(row, CAPACITY)
    quarter = lax.rem(row // CAPACITY, QUARTERS)
    chosen = picked & (rank == slot.astype(jnp.float32)) & (quarter == column // tok)
    tokens_copy.wait()
    for q in range(QUARTERS):
        for j in range(tiles):
            column = (j * QUARTERS + q) * LANES
            cut[q * tok:(q + 1) * tok, j * LANES:(j + 1) * LANES] = tokens_ref[:, column:column + LANES]
    out_ref[...] = jnp.dot(
        chosen.astype(jnp.bfloat16), cut[...], preferred_element_type=jnp.float32
    ).astype(jnp.bfloat16)


def pack(ids, tokens, experts):
    tok, width = tokens.shape
    return pl.pallas_call(
        pack_kernel,
        out_shape=jax.ShapeDtypeStruct((experts * PART, width // QUARTERS), jnp.bfloat16),
        in_specs=[ANYWHERE, ANYWHERE],
        out_specs=VMEM,
        scratch_shapes=[
            pltpu.VMEM(ids.shape, ids.dtype),
            pltpu.VMEM(tokens.shape, tokens.dtype),
            pltpu.VMEM((QUARTERS * tok, width // QUARTERS), jnp.bfloat16),
            pltpu.SemaphoreType.DMA((2,)),
        ],
        compiler_params=pltpu.CompilerParams(vmem_limit_bytes=16 << 20),
    )(ids, tokens)


def weigh(ids_ref, gates_ref, out_ref):
    top, tok = ids_ref.shape
    rows = out_ref.shape[1]
    wide = QUARTERS * tok
    w_of = lax.broadcasted_iota(jnp.int32, (wide, tok), 0)
    t_of = lax.broadcasted_iota(jnp.int32, (wide, tok), 1)
    spread = (lax.rem(w_of, tok) == t_of).astype(jnp.float32)
    contract = (((1,), (1,)), ((), ()))
    ids = lax.dot_general(
        spread, ids_ref[...].astype(jnp.float32), contract, preferred_element_type=jnp.float32
    ).astype(jnp.int32)
    gates = lax.dot_general(
        spread, gates_ref[...], contract,
        precision=lax.Precision.HIGHEST, preferred_element_type=jnp.float32,
    )
    line = lax.broadcasted_iota(jnp.int32, (wide, rows), 0)
    row = lax.broadcasted_iota(jnp.int32, (wide, rows), 1)
    expert = row // PART
    weight = jnp.zeros((wide, rows), jnp.float32)
    picked = jnp.zeros((wide, rows), jnp.float32)
    for k in range(top):
        hit = expert == ids[:, k:k + 1]
        weight = jnp.where(hit, gates[:, k:k + 1], weight)
        picked = jnp.where(hit, 1.0, picked)
    a = lax.broadcasted_iota(jnp.int32, (wide, wide), 0)
    b = lax.broadcasted_iota(jnp.int32, (wide, wide), 1)
    before = ((a // tok == b // tok) & (b < a)).astype(jnp.bfloat16)
    rank = jnp.dot(before, picked.astype(jnp.bfloat16), preferred_element_type=jnp.float32)
    slot = lax.rem(row, CAPACITY)
    quarter = lax.rem(row // CAPACITY, QUARTERS)
    weight = jnp.where((rank == slot.astype(jnp.float32)) & (quarter == line // tok), weight, 0.0)
    high = weight.astype(jnp.bfloat16)
    out_ref[0:wide, :] = high
    out_ref[wide:2 * wide, :] = (weight - high.astype(jnp.float32)).astype(jnp.bfloat16)


def combine_kernel(weights_ref, returned_ref, out_ref):
    tok = out_ref.shape[0]
    wide = QUARTERS * tok
    tiles = returned_ref.shape[1] // LANES
    both = jnp.dot(weights_ref[...], returned_ref[...], preferred_element_type=jnp.float32)
    total = (both[0:wide] + both[wide:2 * wide]).astype(jnp.bfloat16)
    for q in range(QUARTERS):
        for j in range(tiles):
            column = (j * QUARTERS + q) * LANES
            out_ref[:, column:column + LANES] = total[q * tok:(q + 1) * tok, j * LANES:(j + 1) * LANES]


def combine(weights, returned, tok):
    width = returned.shape[1] * QUARTERS
    return pl.pallas_call(
        combine_kernel,
        out_shape=jax.ShapeDtypeStruct((tok, width), jnp.bfloat16),
        in_specs=[VMEM, VMEM],
        out_specs=VMEM,
        compiler_params=pltpu.CompilerParams(vmem_limit_bytes=16 << 20),
    )(weights, returned)


def expert_kernel(
    ids_hbm, gates_hbm, got_ref, gate_hbm, up_hbm, down_hbm, out_ref, weights_ref,
    ids_ref, gates_ref, gate_buf, up_buf, down_buf, wide_buf, rows_buf, hidden_buf,
    small_sem, gate_sem, up_sem, down_sem,
):
    ff_steps, _, ff_tile = gate_buf.shape
    rows, packed = got_ref.shape
    sources = rows // PART
    tiles = packed // LANES
    d_tile = QUARTERS * LANES
    cuts = [tiles * n // DOWN_PARTS for n in range(DOWN_PARTS + 1)]

    def small_copies():
        return (
            pltpu.make_async_copy(ids_hbm, ids_ref, small_sem.at[0]),
            pltpu.make_async_copy(gates_hbm, gates_ref, small_sem.at[1]),
        )

    def in_copies(f):
        part = pl.ds(pl.multiple_of(f * ff_tile, ff_tile), ff_tile)
        return (
            pltpu.make_async_copy(gate_hbm.at[:, part], gate_buf.at[f], gate_sem.at[f]),
            pltpu.make_async_copy(up_hbm.at[:, part], up_buf.at[f], up_sem.at[f]),
        )

    def down_copy(n):
        part = pl.ds(cuts[n] * d_tile, (cuts[n + 1] - cuts[n]) * d_tile)
        return pltpu.make_async_copy(down_hbm.at[:, part], down_buf.at[:, part], down_sem.at[n])

    for copy in small_copies():
        copy.start()
    for f in range(AHEAD):
        for copy in in_copies(f):
            copy.start()

    for j in range(tiles):
        wide_buf[j] = got_ref[:, j * LANES:(j + 1) * LANES].astype(jnp.float32)
    for slot in range(CAPACITY):
        for q in range(QUARTERS):
            for j in range(tiles):
                piece = wide_buf[j, pl.ds(q * CAPACITY + slot, sources, stride=PART), :]
                column = (j * QUARTERS + q) * LANES
                rows_buf[slot * sources:(slot + 1) * sources, column:column + LANES] = piece.astype(jnp.bfloat16)
    for copy in small_copies():
        copy.wait()
    weigh(ids_ref, gates_ref, weights_ref)

    def ff_step(f, carry):
        for copy in in_copies(f):
            copy.wait()

        @pl.when(f + AHEAD < ff_steps)
        def _():
            for copy in in_copies(f + AHEAD):
                copy.start()

        @pl.when(f == 1)
        def _():
            for n in range(DOWN_PARTS):
                down_copy(n).start()

        gate_part = jnp.dot(rows_buf[...], gate_buf[f], preferred_element_type=jnp.float32)
        up_part = jnp.dot(rows_buf[...], up_buf[f], preferred_element_type=jnp.float32)
        hidden_buf[f] = (gate_part / (1.0 + jnp.exp(-gate_part)) * up_part).astype(jnp.bfloat16)
        return carry

    lax.fori_loop(0, ff_steps, ff_step, 0)
    hidden = jnp.concatenate([hidden_buf[f] for f in range(ff_steps)], axis=1)
    for n in range(DOWN_PARTS):
        down_copy(n).wait()
        for j in range(cuts[n], cuts[n + 1]):
            produced = jnp.dot(
                hidden, down_buf[:, j * d_tile:(j + 1) * d_tile], preferred_element_type=jnp.float32
            )
            for slot in range(CAPACITY):
                for q in range(QUARTERS):
                    wide_buf[j, pl.ds(q * CAPACITY + slot, sources, stride=PART), :] = produced[
                        slot * sources:(slot + 1) * sources, q * LANES:(q + 1) * LANES
                    ]
            out_ref[:, j * LANES:(j + 1) * LANES] = wide_buf[j].astype(jnp.bfloat16)


def expert_ffn(ids, gates, got, gate_matrix, up_matrix, down_matrix):
    rows, packed = got.shape
    top, tok = ids.shape
    width, ff = gate_matrix.shape
    ff_steps = ff // FF_TILE
    return pl.pallas_call(
        expert_kernel,
        out_shape=(
            jax.ShapeDtypeStruct(got.shape, jnp.bfloat16),
            jax.ShapeDtypeStruct((2 * QUARTERS * tok, rows), jnp.bfloat16),
        ),
        in_specs=[ANYWHERE, ANYWHERE, VMEM, ANYWHERE, ANYWHERE, ANYWHERE],
        out_specs=(VMEM, VMEM),
        scratch_shapes=[
            pltpu.VMEM(ids.shape, ids.dtype),
            pltpu.VMEM(gates.shape, gates.dtype),
            pltpu.VMEM((ff_steps, width, FF_TILE), jnp.bfloat16),
            pltpu.VMEM((ff_steps, width, FF_TILE), jnp.bfloat16),
            pltpu.VMEM((ff, width), jnp.bfloat16),
            pltpu.VMEM((packed // LANES, rows, LANES), jnp.float32),
            pltpu.VMEM((rows // QUARTERS, width), jnp.bfloat16),
            pltpu.VMEM((ff_steps, rows // QUARTERS, FF_TILE), jnp.bfloat16),
            pltpu.SemaphoreType.DMA((2,)),
            pltpu.SemaphoreType.DMA((ff_steps,)),
            pltpu.SemaphoreType.DMA((ff_steps,)),
            pltpu.SemaphoreType.DMA((DOWN_PARTS,)),
        ],
        compiler_params=pltpu.CompilerParams(vmem_limit_bytes=48 << 20),
    )(ids, gates, got, gate_matrix, up_matrix, down_matrix)


def swap(messages, experts):
    parts = messages.reshape(experts, PART, messages.shape[1])
    moved = lax.all_to_all(parts, ("group", "local"), split_axis=0, concat_axis=0, tiled=True)
    return moved.reshape(messages.shape)


def on_device(tokens, expert_ids, gates, w_gate, w_up, w_down):
    experts = lax.axis_size("group") * lax.axis_size("local")
    ids = expert_ids.T
    got = swap(pack(ids, tokens, experts), experts)
    produced, weights = expert_ffn(ids, gates.T, got, w_gate[0], w_up[0], w_down[0])
    returned = swap(produced, experts)
    return combine(weights, returned, tokens.shape[0])


def solution(mesh):
    placed = (
        P(("group", "local"), None),
        P(("group", "local"), None),
        P(("group", "local"), None),
        P(("group", "local"), None, None),
        P(("group", "local"), None, None),
        P(("group", "local"), None, None),
    )
    return jax.shard_map(
        on_device,
        mesh=mesh,
        in_specs=placed,
        out_specs=P(("group", "local"), None),
        check_vma=False,
    )
```

time: 91.8 us -> 85 us (0.926)
  blocking collectives: 39 us -> 70.8 us
  waiting for transfers between devices: 27.3 us -> 0 us
  Pallas kernels: 19 us -> 12.3 us
  starting transfers between devices: 4.63 us -> 0 us
    all_to_all x1 -> x2, blocking collectives: 39 us -> 70.8 us  [swap(): lax.all_to_all(parts, ('group', 'local'), split_axis=0, concat_axis=0, ti...]
    all_to_all x1 -> x0, waiting for transfers between devices: 27.3 us -> none  [swap(): lax.all_to_all(parts, ('group', 'local'), split_axis=0, concat_axis=0, ti...]
    pallas_call x2 -> x1, Pallas kernels: 16.7 us -> 9.66 us  [expert_ffn(): pl.pallas_call(expert_kernel, out_shape=(jax.ShapeDtypeStruct(got.shape,...]
    all_to_all x1 -> x0, starting transfers between devices: 4.63 us -> none  [swap(): lax.all_to_all(parts, ('group', 'local'), split_axis=0, concat_axis=0, ti...]
  transfers between devices with their start and end apart: 1 -> 0, of which waited for: 1 -> 0; matrix products, arithmetic and copies ran while one was open for 0% -> 0% of each run, Pallas kernels for 1% -> 0%
where the time goes in v2:
time: 85 us; the launch traced here: 84.8 us
  blocking collectives  70.8 us (83%)
  Pallas kernels  12.3 us (14%)
  local copies, waits for them, and re-layouts  1.6 us (2%)
    all_to_all x2, blocking collectives, swap(): lax.all_to_all(parts, ('group', 'local'), split_axis=0, concat_axis=0, ti...  70.8 us
    pallas_call x1, Pallas kernels, expert_ffn(): pl.pallas_call(expert_kernel, out_shape=(jax.ShapeDtypeStruct(got.shape,...  9.66 us

profile of v2, /device:TPU:1, one launch (start us, length us, event | category | flops | bytes accessed | tf_op | source)
XLA Modules:
  0.0 84.8 jit_solution(4816364001927226578)
XLA Ops:
  0.0 0.0 copy-start
  0.0 0.9 %copy-done = bf16[16,3584]{1,0:T(8,128)(2,1)S(1)} copy-done((bf16[16,3584]{1,0:T(8,128)(2,1)S(1)}, bf16[16,3584]{1,0:T(8,128)(2,1)}, u32[]{:S(2)}) %copy-start) | copy-done | bytes 114712
  0.9 0.0 copy-start.1
  0.9 0.7 copy-done.1
  1.6 1.6 %shard_map.64 = bf16[1024,896]{1,0:T(8,128)(2,1)S(1)} custom-call(s32[8,16]{1,0:T(8,128)S(1)} %bitcast.13, bf16[16,3584]{1,0:T(8,128)(2,1)S(1)} %copy-done), custom_call_target="tpu_custom_call" | custom-call | tf_op jit(solution)/shard_map/pallas_call | solution.py:58
  3.2 0.0 copy-start.2
  3.2 0.0 copy-start.3
  3.2 39.0 %all_to_all.10 = bf16[128,8,896]{2,1,0:T(8,128)(2,1)S(1)} all-to-all(bf16[128,8,896]{2,1,0:T(8,128)(2,1)S(1)} %bitcast.10), channel_id=1, replica_groups=mesh['group'=4,'local'=32] {'group','local'}, dimensions={0} | all-to-all | bytes 3670016 | tf_op jit(solution)/shard_map/all_to_all | solution.py:247
  42.2 0.0 copy-done.2
  42.2 0.0 copy-done.3
  42.2 9.7 %shard_map.65 = (bf16[1024,896]{1,0:T(8,128)(2,1)S(1)}, bf16[128,1024]{1,0:T(8,128)(2,1)S(1)}) custom-call(s32[8,16]{1,0:T(8,128)S(1)} %bitcast.14, f32[8,16]{1,0:T(8,128)S(1)} %bitcast.15, bf16[1024,896]{1,0:T(8,128)(2,1)S(1)} %bitcast.11, bf16[3584,1024]{1,0:T(8,128)(2,1)} %bitcast.16, bf16[3584,1024]{1,0:T(8,128)(2,1)} %bitcast.17, ...), custom_call_target="tpu_custom_call" | custom-call | tf_op jit(solution)/shard_map/pallas_call | solution.py:219
  51.9 31.8 %all_to_all.11 = bf16[128,8,896]{2,1,0:T(8,128)(2,1)S(1)} all-to-all(bf16[128,8,896]{2,1,0:T(8,128)(2,1)S(1)} %bitcast.12), channel_id=1, replica_groups=mesh['group'=4,'local'=32] {'group','local'}, dimensions={0} | all-to-all | bytes 3670016 | tf_op jit(solution)/shard_map/all_to_all | solution.py:247
  83.7 1.1 %shard_map.66 = bf16[16,3584]{1,0:T(8,128)(2,1)} custom-call(bf16[128,1024]{1,0:T(8,128)(2,1)S(1)} %get-tuple-element.7.weights_ref, bf16[1024,896]{1,0:T(8,128)(2,1)S(1)} %bitcast.9), custom_call_target="tpu_custom_call" | custom-call | tf_op jit(solution)/shard_map/pallas_call | solution.py:123
Async XLA Ops:
  0.0 0.9 %copy-start = (bf16[16,3584]{1,0:T(8,128)(2,1)S(1)}, bf16[16,3584]{1,0:T(8,128)(2,1)}, u32[]{:S(2)}) copy-start(bf16[16,3584]{1,0:T(8,128)(2,1)} %tokens_hbm.1) | copy-start | bytes 344068
  0.9 0.7 copy-start.1
  3.2 39.0 %copy-start.2 = (s32[16,8]{0,1:T(8,128)S(1)}, s32[16,8]{0,1:T(8,128)}, u32[]{:S(2)}) copy-start(s32[16,8]{0,1:T(8,128)} %param.7) | copy-start | bytes 1540
  3.2 39.0 %copy-start.3 = (f32[16,8]{0,1:T(8,128)S(1)}, f32[16,8]{0,1:T(8,128)}, u32[]{:S(2)}) copy-start(f32[16,8]{0,1:T(8,128)} %param.8) | copy-start | bytes 1540

commit v3 on v1

--- a/solution.py
+++ b/solution.py
@@ -1,5 +1,3 @@
-import functools
-
 import jax
 import jax.numpy as jnp
 from jax import lax
@@ -53,11 +51,12 @@
         in_specs=[VMEM, VMEM],
         out_specs=VMEM,
         scratch_shapes=[pltpu.VMEM((QUARTERS * tok, width // QUARTERS), jnp.bfloat16)],
+        cost_estimate=pl.CostEstimate(flops=8_000_000_000, bytes_accessed=4 << 20, transcendentals=0),
         compiler_params=pltpu.CompilerParams(vmem_limit_bytes=16 << 20),
     )(ids, tokens)
 
 
-def weigh_kernel(ids_ref, gates_ref, out_ref):
+def weigh(ids_ref, gates_ref, out_ref):
     top, tok = ids_ref.shape
     rows = out_ref.shape[1]
     wide = QUARTERS * tok
@@ -93,17 +92,6 @@
     out_ref[wide:2 * wide, :] = (weight - high.astype(jnp.float32)).astype(jnp.bfloat16)
 
 
-def weigh(ids, gates, experts):
-    tok = ids.shape[1]
-    return pl.pallas_call(
-        weigh_kernel,
-        out_shape=jax.ShapeDtypeStruct((2 * QUARTERS * tok, experts * PART), jnp.bfloat16),
-        in_specs=[VMEM, VMEM],
-        out_specs=VMEM,
-        compiler_params=pltpu.CompilerParams(vmem_limit_bytes=16 << 20),
-    )(ids, gates)
-
-
 def combine_kernel(weights_ref, returned_ref, out_ref):
     tok = out_ref.shape[0]
     wide = QUARTERS * tok
@@ -128,49 +116,39 @@
 
 
 def expert_kernel(
-    got_ref, gate_hbm, up_hbm, down_hbm, out_ref,
-    gate_buf, up_buf, down_buf, wide_buf, rows_buf, hidden_buf, gate_sem, up_sem, down_sem,
+    ids_ref, gates_ref, got_ref, gate_ref, up_ref, down_ref, out_ref, weights_ref, wide_buf, rows_buf, hidden_buf
 ):
-    ff_steps, _, ff_tile = gate_buf.shape
-    d_steps, _, d_tile = down_buf.shape
     rows = got_ref.shape[0]
     sources = rows // PART
-
-    def gate_copy(f):
-        return pltpu.make_async_copy(gate_hbm.at[:, pl.ds(f * ff_tile, ff_tile)], gate_buf.at[f], gate_sem.at[f])
-
-    def up_copy(f):
-        return pltpu.make_async_copy(up_hbm.at[:, pl.ds(f * ff_tile, ff_tile)], up_buf.at[f], up_sem.at[f])
-
-    def down_copy(n):
-        return pltpu.make_async_copy(down_hbm.at[:, pl.ds(n * d_tile, d_tile)], down_buf.at[n], down_sem.at[n])
-
-    for f in range(ff_steps):
-        gate_copy(f).start()
-        up_copy(f).start()
-    for n in range(d_steps):
-        down_copy(n).start()
-
-    for j in range(d_steps):
+    tiles = got_ref.shape[1] // LANES
+    ff_tile = 512
+    d_tile = QUARTERS * LANES
+
+    weigh(ids_ref, gates_ref, weights_ref)
+    def unpack(j):
         wide_buf[j] = got_ref[:, j * LANES:(j + 1) * LANES].astype(jnp.float32)
-    for slot in range(CAPACITY):
-        for q in range(QUARTERS):
-            for j in range(d_steps):
+        for slot in range(CAPACITY):
+            for q in range(QUARTERS):
                 piece = wide_buf[j, pl.ds(q * CAPACITY + slot, sources, stride=PART), :]
                 column = (j * QUARTERS + q) * LANES
                 rows_buf[slot * sources:(slot + 1) * sources, column:column + LANES] = piece.astype(jnp.bfloat16)
 
-    for f in range(ff_steps):
-        gate_copy(f).wait()
-        gate_part = jnp.dot(rows_buf[...], gate_buf[f], preferred_element_type=jnp.float32)
-        up_copy(f).wait()
-        up_part = jnp.dot(rows_buf[...], up_buf[f], preferred_element_type=jnp.float32)
+    def product(matrix_ref, part, low, high):
+        return jnp.dot(rows_buf[:, low:high], matrix_ref[low:high, part], preferred_element_type=jnp.float32)
+
+    for j in range(tiles):
+        unpack(j)
+    width = tiles * d_tile
+    for f in range(gate_ref.shape[1] // ff_tile):
+        part = slice(f * ff_tile, (f + 1) * ff_tile)
+        gate_part = product(gate_ref, part, 0, width)
+        up_part = product(up_ref, part, 0, width)
         hidden = gate_part / (1.0 + jnp.exp(-gate_part)) * up_part
-        hidden_buf[:, f * ff_tile:(f + 1) * ff_tile] = hidden.astype(jnp.bfloat16)
-
-    for n in range(d_steps):
-        down_copy(n).wait()
-        produced = jnp.dot(hidden_buf[...], down_buf[n], preferred_element_type=jnp.float32)
+        hidden_buf[:, part] = hidden.astype(jnp.bfloat16)
+    for n in range(tiles):
+        produced = jnp.dot(
+            hidden_buf[...], down_ref[:, n * d_tile:(n + 1) * d_tile], preferred_element_type=jnp.float32
+        )
         for slot in range(CAPACITY):
             for q in range(QUARTERS):
                 wide_buf[n, pl.ds(q * CAPACITY + slot, sources, stride=PART), :] = produced[
@@ -179,31 +157,25 @@
         out_ref[:, n * LANES:(n + 1) * LANES] = wide_buf[n].astype(jnp.bfloat16)
 
 
-def expert_ffn(got, gate_matrix, up_matrix, down_matrix):
-    rows, _ = got.shape
+def expert_ffn(ids, gates, got, gate_matrix, up_matrix, down_matrix):
+    rows, packed = got.shape
     width, ff = gate_matrix.shape
-    ff_tile = 256
-    d_tile = QUARTERS * LANES
-    ff_steps, d_steps = ff // ff_tile, width // d_tile
-    any_spec = pl.BlockSpec(memory_space=pl.ANY)
+    top, tok = ids.shape
     return pl.pallas_call(
         expert_kernel,
-        out_shape=jax.ShapeDtypeStruct(got.shape, jnp.bfloat16),
-        in_specs=[VMEM, any_spec, any_spec, any_spec],
-        out_specs=VMEM,
+        out_shape=(
+            jax.ShapeDtypeStruct(got.shape, jnp.bfloat16),
+            jax.ShapeDtypeStruct((2 * QUARTERS * tok, rows), jnp.bfloat16),
+        ),
+        in_specs=[VMEM] * 6,
+        out_specs=(VMEM, VMEM),
         scratch_shapes=[
-            pltpu.VMEM((ff_steps, width, ff_tile), jnp.bfloat16),
-            pltpu.VMEM((ff_steps, width, ff_tile), jnp.bfloat16),
-            pltpu.VMEM((d_steps, ff, d_tile), jnp.bfloat16),
-            pltpu.VMEM((d_steps, rows, LANES), jnp.float32),
+            pltpu.VMEM((packed // LANES, rows, LANES), jnp.float32),
             pltpu.VMEM((rows // QUARTERS, width), jnp.bfloat16),
             pltpu.VMEM((rows // QUARTERS, ff), jnp.bfloat16),
-            pltpu.SemaphoreType.DMA((ff_steps,)),
-            pltpu.SemaphoreType.DMA((ff_steps,)),
-            pltpu.SemaphoreType.DMA((d_steps,)),
         ],
-        compiler_params=pltpu.CompilerParams(vmem_limit_bytes=48 << 20),
-    )(got, gate_matrix, up_matrix, down_matrix)
+        compiler_params=pltpu.CompilerParams(vmem_limit_bytes=14 << 20),
+    )(ids, gates, got, gate_matrix, up_matrix, down_matrix)
 
 
 def swap(messages, experts):
@@ -216,8 +188,7 @@
     experts = lax.axis_size("group") * lax.axis_size("local")
     ids = expert_ids.T
     got = swap(pack(ids, tokens, experts), experts)
-    produced = expert_ffn(got, w_gate[0], w_up[0], w_down[0])
-    weights = weigh(ids, gates.T, experts)
+    produced, weights = expert_ffn(ids, gates.T, got, w_gate[0], w_up[0], w_down[0])
     returned = swap(produced, experts)
     return combine(weights, returned, tokens.shape[0])
 

time: 91.8 us -> 82.7 us (0.901)
  blocking collectives: 39 us -> 70.8 us
  waiting for transfers between devices: 27.3 us -> 0 us
  Pallas kernels: 19 us -> 9.44 us
  starting transfers between devices: 4.63 us -> 0 us
    all_to_all x1 -> x2, blocking collectives: 39 us -> 70.8 us  [swap(): lax.all_to_all(parts, ('group', 'local'), split_axis=0, concat_axis=0, ti...]
    all_to_all x1 -> x0, waiting for transfers between devices: 27.3 us -> none  [swap(): lax.all_to_all(parts, ('group', 'local'), split_axis=0, concat_axis=0, ti...]
    pallas_call x2 -> x1, Pallas kernels: 16.7 us -> 7.1 us  [expert_ffn(): pl.pallas_call(expert_kernel, out_shape=(jax.ShapeDtypeStruct(got.shape,...]
    all_to_all x1 -> x0, starting transfers between devices: 4.63 us -> none  [swap(): lax.all_to_all(parts, ('group', 'local'), split_axis=0, concat_axis=0, ti...]
    unnamed x8 -> x20, local copies, waits for them, and re-layouts: 1.6 us -> 2.19 us
  transfers between devices with their start and end apart: 1 -> 0, of which waited for: 1 -> 0; matrix products, arithmetic and copies ran while one was open for 0% -> 0% of each run, Pallas kernels for 1% -> 0%
where the time goes in v3:
time: 82.7 us; the launch traced here: 82.5 us
  blocking collectives  70.8 us (86%)
  Pallas kernels  9.44 us (11%)
  local copies, waits for them, and re-layouts  2.19 us (3%)
    all_to_all x2, blocking collectives, swap(): lax.all_to_all(parts, ('group', 'local'), split_axis=0, concat_axis=0, ti...  70.8 us
    pallas_call x1, Pallas kernels, expert_ffn(): pl.pallas_call(expert_kernel, out_shape=(jax.ShapeDtypeStruct(got.shape,...  7.1 us
    unnamed x20, local copies, waits for them, and re-layouts  2.19 us

profile of v3, /device:TPU:1, one launch (start us, length us, event | category | flops | bytes accessed | tf_op | source)
XLA Modules:
  0.0 82.5 jit_solution(10544277227025006311)
XLA Ops:
  0.0 0.0 slice-start
  0.0 0.0 slice-start.2
  0.0 0.0 slice-start.4
  0.0 0.0 copy-start
  0.0 0.8 %copy-done = s32[16,8]{0,1:T(8,128)S(1)} copy-done((s32[16,8]{0,1:T(8,128)S(1)}, s32[16,8]{0,1:T(8,128)}, u32[]{:S(2)}) %copy-start) | copy-done | bytes 536
  0.8 0.0 copy-start.3
  0.9 1.3 %copy-done.3 = bf16[16,3584]{1,0:T(8,128)(2,1)S(1)} copy-done((bf16[16,3584]{1,0:T(8,128)(2,1)S(1)}, bf16[16,3584]{1,0:T(8,128)(2,1)}, u32[]{:S(2)}) %copy-start.3) | copy-done | bytes 114712
  2.2 0.0 slice-start.1
  2.2 0.0 slice-start.3
  2.2 1.2 %shard_map.64 = bf16[1024,896]{1,0:T(8,128)(2,1)S(1)} custom-call(s32[8,16]{1,0:T(8,128)S(1)} %bitcast.22, bf16[16,3584]{1,0:T(8,128)(2,1)S(1)} %copy-done.3), custom_call_target="tpu_custom_call" | custom-call | flops 8000000000 | bytes 4194304 | tf_op jit(solution)/shard_map/pallas_call | solution.py:48
  3.4 0.0 copy-start.1
  3.4 0.0 copy-start.2
  3.4 39.0 %all_to_all.10 = bf16[128,8,896]{2,1,0:T(8,128)(2,1)S(1)} all-to-all(bf16[128,8,896]{2,1,0:T(8,128)(2,1)S(1)} %bitcast.21), channel_id=1, replica_groups=mesh['group'=4,'local'=32] {'group','local'}, dimensions={0} | all-to-all | bytes 3670016 | tf_op jit(solution)/shard_map/all_to_all | solution.py:183
  42.5 0.0 slice-done
  42.5 0.0 slice-done.2
  42.5 0.0 slice-done.4
  42.5 0.0 slice-done.1
  42.5 0.0 slice-done.3
  42.5 0.0 slice-done.5
  42.5 0.0 copy-done.1
  42.5 0.0 copy-done.2
  42.5 7.1 %shard_map.65 = (bf16[1024,896]{1,0:T(8,128)(2,1)S(1)}, bf16[128,1024]{1,0:T(8,128)(2,1)S(1)}) custom-call(s32[8,16]{1,0:T(8,128)S(1)} %bitcast.23, f32[8,16]{1,0:T(8,128)S(1)} %bitcast.24, bf16[1024,896]{1,0:T(8,128)(2,1)S(1)} %bitcast.10, bf16[3584,1024]{1,0:T(8,128)(2,1)S(1)} %bitcast.13, bf16[3584,1024]{1,0:T(8,128)(2,1)S(1)} %bitcast.16, ...), custom_call_target="tpu_custom_call" | custom-call | tf_op jit(solution)/shard_map/pallas_call | solution.py:164
  49.7 31.8 %all_to_all.11 = bf16[128,8,896]{2,1,0:T(8,128)(2,1)S(1)} all-to-all(bf16[128,8,896]{2,1,0:T(8,128)(2,1)S(1)} %bitcast.20), channel_id=1, replica_groups=mesh['group'=4,'local'=32] {'group','local'}, dimensions={0} | all-to-all | bytes 3670016 | tf_op jit(solution)/shard_map/all_to_all | solution.py:183
  81.5 1.1 %shard_map.66 = bf16[16,3584]{1,0:T(8,128)(2,1)} custom-call(bf16[128,1024]{1,0:T(8,128)(2,1)S(1)} %get-tuple-element.7.weights_ref, bf16[1024,896]{1,0:T(8,128)(2,1)S(1)} %bitcast.9), custom_call_target="tpu_custom_call" | custom-call | tf_op jit(solution)/shard_map/pallas_call | solution.py:109
  (4 shorter events, 0.0 us)
Async XLA Ops:
  0.0 42.5 %slice-start = ((s8[7340032]{0:T(1024)(128)(4,1)}), s8[4194304]{0:T(1024)(128)(4,1)S(1)}, s32[]{:S(2)}) async-start(s8[7340032]{0:T(1024)(128)(4,1)} %bitcast.11), calls=%async_computation.2 | async-start | bytes 8388608
  0.0 42.5 %slice-start.2 = ((s8[7340032]{0:T(1024)(128)(4,1)}), s8[4194304]{0:T(1024)(128)(4,1)S(1)}, s32[]{:S(2)}) async-start(s8[7340032]{0:T(1024)(128)(4,1)} %bitcast.14), calls=%async_computation.4 | async-start | bytes 8388608
  0.0 42.5 %slice-start.4 = ((s8[7340032]{0:T(1024)(128)(4,1)}), s8[4194304]{0:T(1024)(128)(4,1)S(1)}, s32[]{:S(2)}) async-start(s8[7340032]{0:T(1024)(128)(4,1)} %bitcast.17), calls=%async_computation.6 | async-start | bytes 8388608
  0.0 0.8 %copy-start = (s32[16,8]{0,1:T(8,128)S(1)}, s32[16,8]{0,1:T(8,128)}, u32[]{:S(2)}) copy-start(s32[16,8]{0,1:T(8,128)} %param.7) | copy-start | bytes 1540
  0.8 1.3 %copy-start.3 = (bf16[16,3584]{1,0:T(8,128)(2,1)S(1)}, bf16[16,3584]{1,0:T(8,128)(2,1)}, u32[]{:S(2)}) copy-start(bf16[16,3584]{1,0:T(8,128)(2,1)} %tokens_ref.1) | copy-start | bytes 344068
  2.2 40.3 %slice-start.1 = ((s8[7340032]{0:T(1024)(128)(4,1)}), s8[3145728]{0:T(1024)(128)(4,1)S(1)}, s32[]{:S(2)}) async-start(s8[7340032]{0:T(1024)(128)(4,1)} %bitcast.11), calls=%async_computation.3 | async-start | bytes 6291456
  2.2 40.3 %slice-start.3 = ((s8[7340032]{0:T(1024)(128)(4,1)}), s8[3145728]{0:T(1024)(128)(4,1)S(1)}, s32[]{:S(2)}) async-start(s8[7340032]{0:T(1024)(128)(4,1)} %bitcast.14), calls=%async_computation.5 | async-start | bytes 6291456
  2.2 40.3 %slice-start.5 = ((s8[7340032]{0:T(1024)(128)(4,1)}), s8[3145728]{0:T(1024)(128)(4,1)S(1)}, s32[]{:S(2)}) async-start(s8[7340032]{0:T(1024)(128)(4,1)} %bitcast.17), calls=%async_computation.7 | async-start | bytes 6291456
  3.4 39.1 %copy-start.1 = (s32[16,8]{0,1:T(8,128)S(1)}, s32[16,8]{0,1:T(8,128)}, u32[]{:S(2)}) copy-start(s32[16,8]{0,1:T(8,128)} %param.7) | copy-start | bytes 1540
  3.4 39.1 %copy-start.2 = (f32[16,8]{0,1:T(8,128)S(1)}, f32[16,8]{0,1:T(8,128)}, u32[]{:S(2)}) copy-start(f32[16,8]{0,1:T(8,128)} %param.8) | copy-start | bytes 1540

commit v4 on v3

--- a/solution.py
+++ b/solution.py
@@ -12,15 +12,9 @@
 VMEM = pl.BlockSpec(memory_space=pltpu.VMEM)
 
 
-def pack_kernel(ids_ref, tokens_ref, out_ref, cut):
+def choose_kernel(ids_ref, out_ref):
     top, tok = ids_ref.shape
-    rows = out_ref.shape[0]
-    tiles = out_ref.shape[1] // LANES
-    wide = QUARTERS * tok
-    for q in range(QUARTERS):
-        for j in range(tiles):
-            column = (j * QUARTERS + q) * LANES
-            cut[q * tok:(q + 1) * tok, j * LANES:(j + 1) * LANES] = tokens_ref[:, column:column + LANES]
+    rows, wide = out_ref.shape
     t_of = lax.broadcasted_iota(jnp.int32, (tok, wide), 0)
     c_of = lax.broadcasted_iota(jnp.int32, (tok, wide), 1)
     spread = (lax.rem(c_of, tok) == t_of).astype(jnp.float32)
@@ -38,22 +32,42 @@
     slot = lax.rem(row, CAPACITY)
     quarter = lax.rem(row // CAPACITY, QUARTERS)
     chosen = picked & (rank == slot.astype(jnp.float32)) & (quarter == column // tok)
-    out_ref[...] = jnp.dot(
-        chosen.astype(jnp.bfloat16), cut[...], preferred_element_type=jnp.float32
-    ).astype(jnp.bfloat16)
-
-
-def pack(ids, tokens, experts):
+    out_ref[...] = chosen.astype(jnp.bfloat16)
+
+
+def choose(ids, experts):
+    tok = ids.shape[1]
+    return pl.pallas_call(
+        choose_kernel,
+        out_shape=jax.ShapeDtypeStruct((experts * PART, QUARTERS * tok), jnp.bfloat16),
+        in_specs=[VMEM],
+        out_specs=VMEM,
+        cost_estimate=pl.CostEstimate(flops=8_000_000_000, bytes_accessed=1 << 18, transcendentals=0),
+        compiler_params=pltpu.CompilerParams(vmem_limit_bytes=8 << 20),
+    )(ids)
+
+
+def pack_kernel(chosen_ref, tokens_ref, out_ref, cut):
+    tok = tokens_ref.shape[0]
+    tiles = out_ref.shape[1] // LANES
+    for q in range(QUARTERS):
+        for j in range(tiles):
+            column = (j * QUARTERS + q) * LANES
+            cut[q * tok:(q + 1) * tok, j * LANES:(j + 1) * LANES] = tokens_ref[:, column:column + LANES]
+    out_ref[...] = jnp.dot(chosen_ref[...], cut[...], preferred_element_type=jnp.float32).astype(jnp.bfloat16)
+
+
+def pack(chosen, tokens):
     tok, width = tokens.shape
     return pl.pallas_call(
         pack_kernel,
-        out_shape=jax.ShapeDtypeStruct((experts * PART, width // QUARTERS), jnp.bfloat16),
+        out_shape=jax.ShapeDtypeStruct((chosen.shape[0], width // QUARTERS), jnp.bfloat16),
         in_specs=[VMEM, VMEM],
         out_specs=VMEM,
         scratch_shapes=[pltpu.VMEM((QUARTERS * tok, width // QUARTERS), jnp.bfloat16)],
         cost_estimate=pl.CostEstimate(flops=8_000_000_000, bytes_accessed=4 << 20, transcendentals=0),
-        compiler_params=pltpu.CompilerParams(vmem_limit_bytes=16 << 20),
-    )(ids, tokens)
+        compiler_params=pltpu.CompilerParams(vmem_limit_bytes=8 << 20),
+    )(chosen, tokens)
 
 
 def weigh(ids_ref, gates_ref, out_ref):
@@ -187,7 +201,7 @@
 def on_device(tokens, expert_ids, gates, w_gate, w_up, w_down):
     experts = lax.axis_size("group") * lax.axis_size("local")
     ids = expert_ids.T
-    got = swap(pack(ids, tokens, experts), experts)
+    got = swap(pack(choose(ids, experts), tokens), experts)
     produced, weights = expert_ffn(ids, gates.T, got, w_gate[0], w_up[0], w_down[0])
     returned = swap(produced, experts)
     return combine(weights, returned, tokens.shape[0])

time: 82.7 us -> 81.3 us (0.983)
  local copies, waits for them, and re-layouts: 2.19 us -> 0.81 us
    unnamed x20, local copies, waits for them, and re-layouts: 2.19 us -> 0.81 us
where the time goes in v4:
time: 81.3 us; the launch traced here: 81.2 us
  blocking collectives  70.8 us (87%)
  Pallas kernels  9.43 us (12%)
    all_to_all x2, blocking collectives, swap(): lax.all_to_all(parts, ('group', 'local'), split_axis=0, concat_axis=0, ti...  70.8 us
    pallas_call x1, Pallas kernels, expert_ffn(): pl.pallas_call(expert_kernel, out_shape=(jax.ShapeDtypeStruct(got.shape,...  6.91 us

profile of v4, /device:TPU:1, one launch (start us, length us, event | category | flops | bytes accessed | tf_op | source)
XLA Modules:
  0.0 81.2 jit_solution(3371135941098042873)
XLA Ops:
  0.0 0.0 copy-start
  0.0 0.7 copy-done
  0.7 0.0 copy-start.3
  0.7 0.0 slice-start
  0.7 0.0 slice-start.2
  0.7 0.0 slice-start.4
  0.7 0.8 shard_map.64.chosen_ref
  1.5 0.1 copy-done.3
  1.6 0.0 slice-start.1
  1.6 0.6 shard_map.65
  2.2 0.0 copy-start.1
  2.2 0.0 copy-start.2
  2.2 39.0 %all_to_all.10 = bf16[128,8,896]{2,1,0:T(8,128)(2,1)S(1)} all-to-all(bf16[128,8,896]{2,1,0:T(8,128)(2,1)S(1)} %bitcast.21), channel_id=1, replica_groups=mesh['group'=4,'local'=32] {'group','local'}, dimensions={0} | all-to-all | bytes 3670016 | tf_op jit(solution)/shard_map/all_to_all | solution.py:197
  41.3 0.0 slice-done
  41.3 0.0 slice-done.2
  41.3 0.0 slice-done.4
  41.3 0.0 slice-done.1
  41.3 0.0 slice-done.3
  41.3 0.0 slice-done.5
  41.3 0.0 copy-done.1
  41.3 0.0 copy-done.2
  41.3 6.9 %shard_map.66 = (bf16[1024,896]{1,0:T(8,128)(2,1)S(1)}, bf16[128,1024]{1,0:T(8,128)(2,1)S(1)}) custom-call(s32[8,16]{1,0:T(8,128)S(1)} %bitcast.23, f32[8,16]{1,0:T(8,128)S(1)} %bitcast.24, bf16[1024,896]{1,0:T(8,128)(2,1)S(1)} %bitcast.10, bf16[3584,1024]{1,0:T(8,128)(2,1)S(1)} %bitcast.13, bf16[3584,1024]{1,0:T(8,128)(2,1)S(1)} %bitcast.16, ...), custom_call_target="tpu_custom_call" | custom-call | tf_op jit(solution)/shard_map/pallas_call | solution.py:178
  48.3 31.8 %all_to_all.11 = bf16[128,8,896]{2,1,0:T(8,128)(2,1)S(1)} all-to-all(bf16[128,8,896]{2,1,0:T(8,128)(2,1)S(1)} %bitcast.20), channel_id=1, replica_groups=mesh['group'=4,'local'=32] {'group','local'}, dimensions={0} | all-to-all | bytes 3670016 | tf_op jit(solution)/shard_map/all_to_all | solution.py:197
  80.1 1.1 %shard_map.67 = bf16[16,3584]{1,0:T(8,128)(2,1)} custom-call(bf16[128,1024]{1,0:T(8,128)(2,1)S(1)} %get-tuple-element.7.weights_ref, bf16[1024,896]{1,0:T(8,128)(2,1)S(1)} %bitcast.9), custom_call_target="tpu_custom_call" | custom-call | tf_op jit(solution)/shard_map/pallas_call | solution.py:123
  (5 shorter events, 0.0 us)
Async XLA Ops:
  0.0 0.7 copy-start
  0.7 0.9 %copy-start.3 = (bf16[16,3584]{1,0:T(8,128)(2,1)S(1)}, bf16[16,3584]{1,0:T(8,128)(2,1)}, u32[]{:S(2)}) copy-start(bf16[16,3584]{1,0:T(8,128)(2,1)} %tokens_ref.1) | copy-start | bytes 344068
  0.7 40.6 %slice-start = ((s8[7340032]{0:T(1024)(128)(4,1)}), s8[4194304]{0:T(1024)(128)(4,1)S(1)}, s32[]{:S(2)}) async-start(s8[7340032]{0:T(1024)(128)(4,1)} %bitcast.11), calls=%async_computation.2 | async-start | bytes 8388608
  0.7 40.6 %slice-start.2 = ((s8[7340032]{0:T(1024)(128)(4,1)}), s8[4194304]{0:T(1024)(128)(4,1)S(1)}, s32[]{:S(2)}) async-start(s8[7340032]{0:T(1024)(128)(4,1)} %bitcast.14), calls=%async_computation.4 | async-start | bytes 8388608
  0.7 40.6 %slice-start.4 = ((s8[7340032]{0:T(1024)(128)(4,1)}), s8[4194304]{0:T(1024)(128)(4,1)S(1)}, s32[]{:S(2)}) async-start(s8[7340032]{0:T(1024)(128)(4,1)} %bitcast.17), calls=%async_computation.6 | async-start | bytes 8388608
  1.6 39.7 %slice-start.1 = ((s8[7340032]{0:T(1024)(128)(4,1)}), s8[3145728]{0:T(1024)(128)(4,1)S(1)}, s32[]{:S(2)}) async-start(s8[7340032]{0:T(1024)(128)(4,1)} %bitcast.11), calls=%async_computation.3 | async-start | bytes 6291456
  1.6 39.7 %slice-start.3 = ((s8[7340032]{0:T(1024)(128)(4,1)}), s8[3145728]{0:T(1024)(128)(4,1)S(1)}, s32[]{:S(2)}) async-start(s8[7340032]{0:T(1024)(128)(4,1)} %bitcast.14), calls=%async_computation.5 | async-start | bytes 6291456
  1.6 39.7 %slice-start.5 = ((s8[7340032]{0:T(1024)(128)(4,1)}), s8[3145728]{0:T(1024)(128)(4,1)S(1)}, s32[]{:S(2)}) async-start(s8[7340032]{0:T(1024)(128)(4,1)} %bitcast.17), calls=%async_computation.7 | async-start | bytes 6291456
  2.2 39.1 %copy-start.1 = (s32[16,8]{0,1:T(8,128)S(1)}, s32[16,8]{0,1:T(8,128)}, u32[]{:S(2)}) copy-start(s32[16,8]{0,1:T(8,128)} %param.7) | copy-start | bytes 1540
  2.2 39.1 %copy-start.2 = (f32[16,8]{0,1:T(8,128)S(1)}, f32[16,8]{0,1:T(8,128)}, u32[]{:S(2)}) copy-start(f32[16,8]{0,1:T(8,128)} %param.8) | copy-start | bytes 1540

commit v5 on v4

v5 whole, which is shorter than its diff:
```python
import jax
import jax.numpy as jnp
from jax import lax
from jax.experimental import pallas as pl
from jax.experimental.pallas import tpu as pltpu
from jax.sharding import PartitionSpec as P

CAPACITY = 2
QUARTERS = 4
PART = CAPACITY * QUARTERS
LANES = 128
VMEM = pl.BlockSpec(memory_space=pltpu.VMEM)


def turned(values):
    tok = values.shape[1]
    a = lax.broadcasted_iota(jnp.int32, (tok, tok), 0)
    b = lax.broadcasted_iota(jnp.int32, (tok, tok), 1)
    return lax.dot_general(
        (a == b).astype(jnp.float32), values, (((1,), (1,)), ((), ())),
        precision=lax.Precision.HIGHEST, preferred_element_type=jnp.float32,
    )


def choose_kernel(ids_ref, out_ref):
    top, tok = ids_ref.shape
    rows = out_ref.shape[1]
    ids = turned(ids_ref[...]).astype(jnp.int32)
    row = lax.broadcasted_iota(jnp.int32, (tok, rows), 1)
    expert = row // PART
    picked = expert == ids[:, 0:1]
    for k in range(1, top):
        picked = picked | (expert == ids[:, k:k + 1])
    a = lax.broadcasted_iota(jnp.int32, (tok, tok), 0)
    b = lax.broadcasted_iota(jnp.int32, (tok, tok), 1)
    before = (b < a).astype(jnp.bfloat16)
    rank = jnp.dot(before, picked.astype(jnp.bfloat16), preferred_element_type=jnp.float32)
    slot = lax.rem(row, CAPACITY)
    quarter = lax.rem(row // CAPACITY, QUARTERS)
    chosen = picked & (rank == slot.astype(jnp.float32))
    for q in range(QUARTERS):
        out_ref[q * tok:(q + 1) * tok, :] = (chosen & (quarter == q)).astype(jnp.bfloat16)


def choose(ids, experts):
    tok = ids.shape[1]
    return pl.pallas_call(
        choose_kernel,
        out_shape=jax.ShapeDtypeStruct((QUARTERS * tok, experts * PART), jnp.bfloat16),
        in_specs=[VMEM],
        out_specs=VMEM,
        cost_estimate=pl.CostEstimate(flops=8_000_000_000, bytes_accessed=1 << 18, transcendentals=0),
        compiler_params=pltpu.CompilerParams(vmem_limit_bytes=8 << 20),
    )(ids)


def pack_kernel(chosen_ref, tokens_ref, out_ref, cut):
    tok = tokens_ref.shape[0]
    tiles = out_ref.shape[1] // LANES
    for q in range(QUARTERS):
        for j in range(tiles):
            column = (j * QUARTERS + q) * LANES
            cut[q * tok:(q + 1) * tok, j * LANES:(j + 1) * LANES] = tokens_ref[:, column:column + LANES]
    out_ref[...] = lax.dot_general(
        chosen_ref[...], cut[...], (((0,), (0,)), ((), ())), preferred_element_type=jnp.float32
    ).astype(jnp.bfloat16)


def pack(chosen, tokens):
    tok, width = tokens.shape
    return pl.pallas_call(
        pack_kernel,
        out_shape=jax.ShapeDtypeStruct((chosen.shape[1], width // QUARTERS), jnp.bfloat16),
        in_specs=[VMEM, VMEM],
        out_specs=VMEM,
        scratch_shapes=[pltpu.VMEM((QUARTERS * tok, width // QUARTERS), jnp.bfloat16)],
        cost_estimate=pl.CostEstimate(flops=8_000_000_000, bytes_accessed=4 << 20, transcendentals=0),
        compiler_params=pltpu.CompilerParams(vmem_limit_bytes=8 << 20),
    )(chosen, tokens)


def weigh(ids_ref, gates_ref, chosen_ref, out_ref):
    top, tok = ids_ref.shape
    rows = out_ref.shape[1]
    wide = QUARTERS * tok
    ids = turned(ids_ref[...]).astype(jnp.int32)
    gates = turned(gates_ref[...])
    expert = lax.broadcasted_iota(jnp.int32, (tok, rows), 1) // PART
    weight = jnp.zeros((tok, rows), jnp.float32)
    for k in range(top):
        weight = jnp.where(expert == ids[:, k:k + 1], gates[:, k:k + 1], weight)
    high = weight.astype(jnp.bfloat16)
    low = (weight - high.astype(jnp.float32)).astype(jnp.bfloat16)
    for q in range(QUARTERS):
        part = slice(q * tok, (q + 1) * tok)
        chosen = chosen_ref[part, :]
        out_ref[part, :] = high * chosen
        out_ref[wide + q * tok:wide + (q + 1) * tok, :] = low * chosen


def combine_kernel(weights_ref, returned_ref, out_ref):
    tok = out_ref.shape[0]
    wide = QUARTERS * tok
    tiles = returned_ref.shape[1] // LANES
    both = jnp.dot(weights_ref[...], returned_ref[...], preferred_element_type=jnp.float32)
    total = (both[0:wide] + both[wide:2 * wide]).astype(jnp.bfloat16)
    for q in range(QUARTERS):
        for j in range(tiles):
            column = (j * QUARTERS + q) * LANES
            out_ref[:, column:column + LANES] = total[q * tok:(q + 1) * tok, j * LANES:(j + 1) * LANES]


def combine(weights, returned, tok):
    width = returned.shape[1] * QUARTERS
    return pl.pallas_call(
        combine_kernel,
        out_shape=jax.ShapeDtypeStruct((tok, width), jnp.bfloat16),
        in_specs=[VMEM, VMEM],
        out_specs=VMEM,
        compiler_params=pltpu.CompilerParams(vmem_limit_bytes=16 << 20),
    )(weights, returned)


def expert_kernel(
    ids_ref, gates_ref, chosen_ref, got_ref, gate_ref, up_ref, down_ref, out_ref, weights_ref, wide_buf, rows_buf, hidden_buf
):
    rows = got_ref.shape[0]
    sources = rows // PART
    tiles = got_ref.shape[1] // LANES
    ff_tile = 512
    d_tile = QUARTERS * LANES

    weigh(ids_ref, gates_ref, chosen_ref, weights_ref)
    def unpack(j):
        wide_buf[j] = got_ref[:, j * LANES:(j + 1) * LANES].astype(jnp.float32)
        for slot in range(CAPACITY):
            for q in range(QUARTERS):
                piece = wide_buf[j, pl.ds(q * CAPACITY + slot, sources, stride=PART), :]
                column = (j * QUARTERS + q) * LANES
                rows_buf[slot * sources:(slot + 1) * sources, column:column + LANES] = piece.astype(jnp.bfloat16)

    def product(matrix_ref, part, low, high):
        return jnp.dot(rows_buf[:, low:high], matrix_ref[low:high, part], preferred_element_type=jnp.float32)

    for j in range(tiles):
        unpack(j)
    width = tiles * d_tile
    for f in range(gate_ref.shape[1] // ff_tile):
        part = slice(f * ff_tile, (f + 1) * ff_tile)
        gate_part = product(gate_ref, part, 0, width)
        up_part = product(up_ref, part, 0, width)
        hidden = gate_part / (1.0 + jnp.exp(-gate_part)) * up_part
        hidden_buf[:, part] = hidden.astype(jnp.bfloat16)
    for n in range(tiles):
        produced = jnp.dot(
            hidden_buf[...], down_ref[:, n * d_tile:(n + 1) * d_tile], preferred_element_type=jnp.float32
        )
        for slot in range(CAPACITY):
            for q in range(QUARTERS):
                wide_buf[n, pl.ds(q * CAPACITY + slot, sources, stride=PART), :] = produced[
                    slot * sources:(slot + 1) * sources, q * LANES:(q + 1) * LANES
                ]
        out_ref[:, n * LANES:(n + 1) * LANES] = wide_buf[n].astype(jnp.bfloat16)


def expert_ffn(ids, gates, chosen, got, gate_matrix, up_matrix, down_matrix):
    rows, packed = got.shape
    width, ff = gate_matrix.shape
    top, tok = ids.shape
    return pl.pallas_call(
        expert_kernel,
        out_shape=(
            jax.ShapeDtypeStruct(got.shape, jnp.bfloat16),
            jax.ShapeDtypeStruct((2 * QUARTERS * tok, rows), jnp.bfloat16),
        ),
        in_specs=[VMEM] * 7,
        out_specs=(VMEM, VMEM),
        scratch_shapes=[
            pltpu.VMEM((packed // LANES, rows, LANES), jnp.float32),
            pltpu.VMEM((rows // QUARTERS, width), jnp.bfloat16),
            pltpu.VMEM((rows // QUARTERS, ff), jnp.bfloat16),
        ],
        compiler_params=pltpu.CompilerParams(vmem_limit_bytes=14 << 20),
    )(ids, gates, chosen, got, gate_matrix, up_matrix, down_matrix)


def swap(messages, experts):
    parts = messages.reshape(experts, PART, messages.shape[1])
    moved = lax.all_to_all(parts, ("group", "local"), split_axis=0, concat_axis=0, tiled=True)
    return moved.reshape(messages.shape)


def on_device(tokens, expert_ids, gates, w_gate, w_up, w_down):
    experts = lax.axis_size("group") * lax.axis_size("local")
    ids = expert_ids.T.astype(jnp.float32)
    chosen = choose(ids, experts)
    got = swap(pack(chosen, tokens), experts)
    produced, weights = expert_ffn(ids, gates.T, chosen, got, w_gate[0], w_up[0], w_down[0])
    returned = swap(produced, experts)
    return combine(weights, returned, tokens.shape[0])


def solution(mesh):
    placed = (
        P(("group", "local"), None),
        P(("group", "local"), None),
        P(("group", "local"), None),
        P(("group", "local"), None, None),
        P(("group", "local"), None, None),
        P(("group", "local"), None, None),
    )
    return jax.shard_map(
        on_device,
        mesh=mesh,
        in_specs=placed,
        out_specs=P(("group", "local"), None),
        check_vma=False,
    )
```

time: 81.3 us -> 81.1 us (level)
  no operation moved by 1% of the time
where the time goes in v5:
time: 81.1 us; the launch traced here: 80.9 us
  blocking collectives  70.8 us (87%)
  Pallas kernels  8.82 us (11%)
    all_to_all x2, blocking collectives, swap(): lax.all_to_all(parts, ('group', 'local'), split_axis=0, concat_axis=0, ti...  70.8 us
    pallas_call x1, Pallas kernels, expert_ffn(): pl.pallas_call(expert_kernel, out_shape=(jax.ShapeDtypeStruct(got.shape,...  6.66 us

profile of v5, /device:TPU:1, one launch (start us, length us, event | category | flops | bytes accessed | tf_op | source)
XLA Modules:
  0.0 80.9 jit_solution(2859109045837943534)
XLA Ops:
  0.0 0.7 convert_bitcast_fusion.ids_ref
  0.7 0.0 copy-start.1
  0.7 0.0 slice-start
  0.7 0.0 slice-start.2
  0.7 0.0 slice-start.4
  0.7 0.4 shard_map.64.chosen_ref
  1.1 0.5 copy-done.1
  1.6 0.0 slice-start.1
  1.6 0.0 slice-start.3
  1.6 0.0 slice-start.5
  1.6 0.7 shard_map.65
  2.3 0.0 copy-start
  2.3 39.0 %all_to_all.10 = bf16[128,8,896]{2,1,0:T(8,128)(2,1)S(1)} all-to-all(bf16[128,8,896]{2,1,0:T(8,128)(2,1)S(1)} %bitcast.22), channel_id=1, replica_groups=mesh['group'=4,'local'=32] {'group','local'}, dimensions={0} | all-to-all | bytes 3670016 | tf_op jit(solution)/shard_map/all_to_all | solution.py:189
  41.3 0.0 slice-done
  41.3 0.0 slice-done.2
  41.3 0.0 slice-done.4
  41.3 0.0 slice-done.1
  41.3 0.0 slice-done.3
  41.3 0.0 slice-done.5
  41.3 0.0 copy-done
  41.4 6.7 %shard_map.66 = (bf16[1024,896]{1,0:T(8,128)(2,1)S(1)}, bf16[128,1024]{1,0:T(8,128)(2,1)S(1)}) custom-call(f32[8,16]{1,0:T(8,128)S(1)} %convert_bitcast_fusion.ids_ref, f32[8,16]{1,0:T(8,128)S(1)} %bitcast.23, bf16[64,1024]{1,0:T(8,128)(2,1)S(1)} %shard_map.64.chosen_ref, bf16[1024,896]{1,0:T(8,128)(2,1)S(1)} %bitcast.20, bf16[3584,1024]{1,0:T(8,128)(2,1)S(1)} %bitcast.13, ...), custom_call_target="tpu_custom_call" | custom-call | tf_op jit(solution)/shard_map/pallas_call | solution.py:170
  48.0 31.8 %all_to_all.11 = bf16[128,8,896]{2,1,0:T(8,128)(2,1)S(1)} all-to-all(bf16[128,8,896]{2,1,0:T(8,128)(2,1)S(1)} %bitcast.21), channel_id=1, replica_groups=mesh['group'=4,'local'=32] {'group','local'}, dimensions={0} | all-to-all | bytes 3670016 | tf_op jit(solution)/shard_map/all_to_all | solution.py:189
  79.8 1.1 %shard_map.67 = bf16[16,3584]{1,0:T(8,128)(2,1)} custom-call(bf16[128,1024]{1,0:T(8,128)(2,1)S(1)} %get-tuple-element.7.weights_ref, bf16[1024,896]{1,0:T(8,128)(2,1)S(1)} %bitcast.10), custom_call_target="tpu_custom_call" | custom-call | tf_op jit(solution)/shard_map/pallas_call | solution.py:115
  (3 shorter events, 0.0 us)
Async XLA Ops:
  0.7 0.9 %copy-start.1 = (bf16[16,3584]{1,0:T(8,128)(2,1)S(1)}, bf16[16,3584]{1,0:T(8,128)(2,1)}, u32[]{:S(2)}) copy-start(bf16[16,3584]{1,0:T(8,128)(2,1)} %tokens_ref.1) | copy-start | bytes 344068
  0.7 40.6 %slice-start = ((s8[7340032]{0:T(1024)(128)(4,1)}), s8[4194304]{0:T(1024)(128)(4,1)S(1)}, s32[]{:S(2)}) async-start(s8[7340032]{0:T(1024)(128)(4,1)} %bitcast.11), calls=%async_computation.2 | async-start | bytes 8388608
  0.7 40.6 %slice-start.2 = ((s8[7340032]{0:T(1024)(128)(4,1)}), s8[4194304]{0:T(1024)(128)(4,1)S(1)}, s32[]{:S(2)}) async-start(s8[7340032]{0:T(1024)(128)(4,1)} %bitcast.14), calls=%async_computation.4 | async-start | bytes 8388608
  0.7 40.6 %slice-start.4 = ((s8[7340032]{0:T(1024)(128)(4,1)}), s8[4194304]{0:T(1024)(128)(4,1)S(1)}, s32[]{:S(2)}) async-start(s8[7340032]{0:T(1024)(128)(4,1)} %bitcast.17), calls=%async_computation.6 | async-start | bytes 8388608
  1.6 39.7 %slice-start.1 = ((s8[7340032]{0:T(1024)(128)(4,1)}), s8[3145728]{0:T(1024)(128)(4,1)S(1)}, s32[]{:S(2)}) async-start(s8[7340032]{0:T(1024)(128)(4,1)} %bitcast.11), calls=%async_computation.3 | async-start | bytes 6291456
  1.6 39.7 %slice-start.3 = ((s8[7340032]{0:T(1024)(128)(4,1)}), s8[3145728]{0:T(1024)(128)(4,1)S(1)}, s32[]{:S(2)}) async-start(s8[7340032]{0:T(1024)(128)(4,1)} %bitcast.14), calls=%async_computation.5 | async-start | bytes 6291456
  1.6 39.7 %slice-start.5 = ((s8[7340032]{0:T(1024)(128)(4,1)}), s8[3145728]{0:T(1024)(128)(4,1)S(1)}, s32[]{:S(2)}) async-start(s8[7340032]{0:T(1024)(128)(4,1)} %bitcast.17), calls=%async_computation.7 | async-start | bytes 6291456
  2.3 39.1 %copy-start = (f32[16,8]{0,1:T(8,128)S(1)}, f32[16,8]{0,1:T(8,128)}, u32[]{:S(2)}) copy-start(f32[16,8]{0,1:T(8,128)} %param.8) | copy-start | bytes 1540

commit v6 on v5

--- a/solution.py
+++ b/solution.py
@@ -122,39 +122,41 @@
 
 
 def expert_kernel(
-    ids_ref, gates_ref, chosen_ref, got_ref, gate_ref, up_ref, down_ref, out_ref, weights_ref, wide_buf, rows_buf, hidden_buf
+    ids_ref, gates_ref, chosen_ref, got_ref, gate_ref, up_ref, down_ref, out_ref, weights_ref, wide_buf
 ):
     rows = got_ref.shape[0]
     sources = rows // PART
     tiles = got_ref.shape[1] // LANES
-    ff_tile = 512
     d_tile = QUARTERS * LANES
 
     weigh(ids_ref, gates_ref, chosen_ref, weights_ref)
+
     def unpack(j):
         wide_buf[j] = got_ref[:, j * LANES:(j + 1) * LANES].astype(jnp.float32)
-        for slot in range(CAPACITY):
-            for q in range(QUARTERS):
-                piece = wide_buf[j, pl.ds(q * CAPACITY + slot, sources, stride=PART), :]
-                column = (j * QUARTERS + q) * LANES
-                rows_buf[slot * sources:(slot + 1) * sources, column:column + LANES] = piece.astype(jnp.bfloat16)
-
-    def product(matrix_ref, part, low, high):
-        return jnp.dot(rows_buf[:, low:high], matrix_ref[low:high, part], preferred_element_type=jnp.float32)
-
+        return jnp.concatenate(
+            [
+                jnp.concatenate(
+                    [
+                        wide_buf[j, pl.ds(q * CAPACITY + slot, sources, stride=PART), :].astype(jnp.bfloat16)
+                        for q in range(QUARTERS)
+                    ],
+                    axis=1,
+                )
+                for slot in range(CAPACITY)
+            ],
+            axis=0,
+        )
+
+    gate_part = up_part = 0.0
     for j in range(tiles):
-        unpack(j)
-    width = tiles * d_tile
-    for f in range(gate_ref.shape[1] // ff_tile):
-        part = slice(f * ff_tile, (f + 1) * ff_tile)
-        gate_part = product(gate_ref, part, 0, width)
-        up_part = product(up_ref, part, 0, width)
-        hidden = gate_part / (1.0 + jnp.exp(-gate_part)) * up_part
-        hidden_buf[:, part] = hidden.astype(jnp.bfloat16)
-    for n in range(tiles):
-        produced = jnp.dot(
-            hidden_buf[...], down_ref[:, n * d_tile:(n + 1) * d_tile], preferred_element_type=jnp.float32
-        )
+        piece = unpack(j)
+        part = slice(j * d_tile, (j + 1) * d_tile)
+        gate_part += jnp.dot(piece, gate_ref[part, :], preferred_element_type=jnp.float32)
+        up_part += jnp.dot(piece, up_ref[part, :], preferred_element_type=jnp.float32)
+    hidden = gate_part / (1.0 + jnp.exp(-gate_part)) * up_part
+    hidden = hidden.astype(jnp.bfloat16)
+
+    def scatter(n, produced):
         for slot in range(CAPACITY):
             for q in range(QUARTERS):
                 wide_buf[n, pl.ds(q * CAPACITY + slot, sources, stride=PART), :] = produced[
@@ -162,10 +164,17 @@
                 ]
         out_ref[:, n * LANES:(n + 1) * LANES] = wide_buf[n].astype(jnp.bfloat16)
 
+    before = None
+    for n in range(tiles):
+        produced = jnp.dot(hidden, down_ref[:, n * d_tile:(n + 1) * d_tile], preferred_element_type=jnp.float32)
+        if before is not None:
+            scatter(n - 1, before)
+        before = produced
+    scatter(tiles - 1, before)
+
 
 def expert_ffn(ids, gates, chosen, got, gate_matrix, up_matrix, down_matrix):
     rows, packed = got.shape
-    width, ff = gate_matrix.shape
     top, tok = ids.shape
     return pl.pallas_call(
         expert_kernel,
@@ -177,8 +186,6 @@
         out_specs=(VMEM, VMEM),
         scratch_shapes=[
             pltpu.VMEM((packed // LANES, rows, LANES), jnp.float32),
-            pltpu.VMEM((rows // QUARTERS, width), jnp.bfloat16),
-            pltpu.VMEM((rows // QUARTERS, ff), jnp.bfloat16),
         ],
         compiler_params=pltpu.CompilerParams(vmem_limit_bytes=14 << 20),
     )(ids, gates, chosen, got, gate_matrix, up_matrix, down_matrix)

time: 81.1 us -> 80.8 us (level)
  no operation moved by 1% of the time
where the time goes in v6:
time: 80.8 us; the launch traced here: 80.7 us
  blocking collectives  70.8 us (88%)
  Pallas kernels  8.53 us (11%)
    all_to_all x2, blocking collectives, swap(): lax.all_to_all(parts, ('group', 'local'), split_axis=0, concat_axis=0, ti...  70.8 us
    pallas_call x1, Pallas kernels, expert_ffn(): pl.pallas_call(expert_kernel, out_shape=(jax.ShapeDtypeStruct(got.shape,...  6.36 us

profile of v6, /device:TPU:1, one launch (start us, length us, event | category | flops | bytes accessed | tf_op | source)
XLA Modules:
  0.0 80.7 jit_solution(4245049031913248570)
XLA Ops:
  0.0 0.7 convert_bitcast_fusion.ids_ref
  0.7 0.0 copy-start.1
  0.7 0.0 slice-start
  0.7 0.0 slice-start.2
  0.7 0.0 slice-start.4
  0.7 0.4 shard_map.64.chosen_ref
  1.1 0.5 copy-done.1
  1.6 0.0 slice-start.1
  1.6 0.0 slice-start.3
  1.6 0.0 slice-start.5
  1.6 0.7 shard_map.65
  2.3 0.0 copy-start
  2.3 39.0 %all_to_all.10 = bf16[128,8,896]{2,1,0:T(8,128)(2,1)S(1)} all-to-all(bf16[128,8,896]{2,1,0:T(8,128)(2,1)S(1)} %bitcast.22), channel_id=1, replica_groups=mesh['group'=4,'local'=32] {'group','local'}, dimensions={0} | all-to-all | bytes 3670016 | tf_op jit(solution)/shard_map/all_to_all | solution.py:196
  41.3 0.0 slice-done
  41.3 0.0 slice-done.2
  41.3 0.0 slice-done.4
  41.3 0.0 slice-done.1
  41.3 0.0 slice-done.3
  41.3 0.0 slice-done.5
  41.3 0.0 copy-done
  41.4 6.4 %shard_map.66 = (bf16[1024,896]{1,0:T(8,128)(2,1)S(1)}, bf16[128,1024]{1,0:T(8,128)(2,1)S(1)}) custom-call(f32[8,16]{1,0:T(8,128)S(1)} %convert_bitcast_fusion.ids_ref, f32[8,16]{1,0:T(8,128)S(1)} %bitcast.23, bf16[64,1024]{1,0:T(8,128)(2,1)S(1)} %shard_map.64.chosen_ref, bf16[1024,896]{1,0:T(8,128)(2,1)S(1)} %bitcast.20, bf16[3584,1024]{1,0:T(8,128)(2,1)S(1)} %bitcast.13, ...), custom_call_target="tpu_custom_call" | custom-call | tf_op jit(solution)/shard_map/pallas_call | solution.py:179
  47.7 31.8 %all_to_all.11 = bf16[128,8,896]{2,1,0:T(8,128)(2,1)S(1)} all-to-all(bf16[128,8,896]{2,1,0:T(8,128)(2,1)S(1)} %bitcast.21), channel_id=1, replica_groups=mesh['group'=4,'local'=32] {'group','local'}, dimensions={0} | all-to-all | bytes 3670016 | tf_op jit(solution)/shard_map/all_to_all | solution.py:196
  79.6 1.1 %shard_map.67 = bf16[16,3584]{1,0:T(8,128)(2,1)} custom-call(bf16[128,1024]{1,0:T(8,128)(2,1)S(1)} %get-tuple-element.7.weights_ref, bf16[1024,896]{1,0:T(8,128)(2,1)S(1)} %bitcast.10), custom_call_target="tpu_custom_call" | custom-call | tf_op jit(solution)/shard_map/pallas_call | solution.py:115
  (3 shorter events, 0.0 us)
Async XLA Ops:
  0.7 0.9 %copy-start.1 = (bf16[16,3584]{1,0:T(8,128)(2,1)S(1)}, bf16[16,3584]{1,0:T(8,128)(2,1)}, u32[]{:S(2)}) copy-start(bf16[16,3584]{1,0:T(8,128)(2,1)} %tokens_ref.1) | copy-start | bytes 344068
  0.7 40.6 %slice-start = ((s8[7340032]{0:T(1024)(128)(4,1)}), s8[4194304]{0:T(1024)(128)(4,1)S(1)}, s32[]{:S(2)}) async-start(s8[7340032]{0:T(1024)(128)(4,1)} %bitcast.11), calls=%async_computation.2 | async-start | bytes 8388608
  0.7 40.6 %slice-start.2 = ((s8[7340032]{0:T(1024)(128)(4,1)}), s8[4194304]{0:T(1024)(128)(4,1)S(1)}, s32[]{:S(2)}) async-start(s8[7340032]{0:T(1024)(128)(4,1)} %bitcast.14), calls=%async_computation.4 | async-start | bytes 8388608
  0.7 40.6 %slice-start.4 = ((s8[7340032]{0:T(1024)(128)(4,1)}), s8[4194304]{0:T(1024)(128)(4,1)S(1)}, s32[]{:S(2)}) async-start(s8[7340032]{0:T(1024)(128)(4,1)} %bitcast.17), calls=%async_computation.6 | async-start | bytes 8388608
  1.6 39.7 %slice-start.1 = ((s8[7340032]{0:T(1024)(128)(4,1)}), s8[3145728]{0:T(1024)(128)(4,1)S(1)}, s32[]{:S(2)}) async-start(s8[7340032]{0:T(1024)(128)(4,1)} %bitcast.11), calls=%async_computation.3 | async-start | bytes 6291456
  1.6 39.7 %slice-start.3 = ((s8[7340032]{0:T(1024)(128)(4,1)}), s8[3145728]{0:T(1024)(128)(4,1)S(1)}, s32[]{:S(2)}) async-start(s8[7340032]{0:T(1024)(128)(4,1)} %bitcast.14), calls=%async_computation.5 | async-start | bytes 6291456
  1.6 39.7 %slice-start.5 = ((s8[7340032]{0:T(1024)(128)(4,1)}), s8[3145728]{0:T(1024)(128)(4,1)S(1)}, s32[]{:S(2)}) async-start(s8[7340032]{0:T(1024)(128)(4,1)} %bitcast.17), calls=%async_computation.7 | async-start | bytes 6291456
  2.3 39.1 %copy-start = (f32[16,8]{0,1:T(8,128)S(1)}, f32[16,8]{0,1:T(8,128)}, u32[]{:S(2)}) copy-start(f32[16,8]{0,1:T(8,128)} %param.8) | copy-start | bytes 1540

commit v7 on v6

--- a/solution.py
+++ b/solution.py
@@ -9,6 +9,7 @@
 QUARTERS = 4
 PART = CAPACITY * QUARTERS
 LANES = 128
+ORDER = [x * 32 + y * 8 + z * 2 + c for c in range(2) for z in range(4) for y in range(4) for x in range(4)]
 VMEM = pl.BlockSpec(memory_space=pltpu.VMEM)
 
 
@@ -193,13 +194,15 @@
 
 def swap(messages, experts):
     parts = messages.reshape(experts, PART, messages.shape[1])
-    moved = lax.all_to_all(parts, ("group", "local"), split_axis=0, concat_axis=0, tiled=True)
+    moved = lax.all_to_all(parts, ("group", "local"), axis_index_groups=[ORDER], split_axis=0, concat_axis=0, tiled=True)
     return moved.reshape(messages.shape)
 
 
 def on_device(tokens, expert_ids, gates, w_gate, w_up, w_down):
     experts = lax.axis_size("group") * lax.axis_size("local")
-    ids = expert_ids.T.astype(jnp.float32)
+    e = expert_ids
+    message = (e & 1) * 64 + ((e >> 1) & 3) * 16 + ((e >> 3) & 3) * 4 + (e >> 5)
+    ids = message.T.astype(jnp.float32)
     chosen = choose(ids, experts)
     got = swap(pack(chosen, tokens), experts)
     produced, weights = expert_ffn(ids, gates.T, chosen, got, w_gate[0], w_up[0], w_down[0])

time: 80.8 us -> 78.9 us (0.976)
  blocking collectives: 70.8 us -> 68.9 us
    all_to_all x2, blocking collectives: 70.8 us -> 68.9 us  [swap(): lax.all_to_all(parts, ('group', 'local'), axis_index_groups=[ORDER], spli...]
where the time goes in v7:
time: 78.9 us; the launch traced here: 78.7 us
  blocking collectives  68.9 us (87%)
  Pallas kernels  8.54 us (11%)
    all_to_all x2, blocking collectives, swap(): lax.all_to_all(parts, ('group', 'local'), axis_index_groups=[ORDER], spli...  68.9 us
    pallas_call x1, Pallas kernels, expert_ffn(): pl.pallas_call(expert_kernel, out_shape=(jax.ShapeDtypeStruct(got.shape,...  6.38 us

profile of v7, /device:TPU:1, one launch (start us, length us, event | category | flops | bytes accessed | tf_op | source)
XLA Modules:
  0.0 78.7 jit_solution(2505283082810670685)
XLA Ops:
  0.0 0.7 convert_bitcast_fusion.ids_ref
  0.7 0.0 copy-start.1
  0.7 0.0 slice-start
  0.7 0.0 slice-start.2
  0.7 0.0 slice-start.4
  0.7 0.4 shard_map.64.chosen_ref
  1.1 0.5 copy-done.1
  1.6 0.0 slice-start.1
  1.6 0.0 slice-start.3
  1.6 0.0 slice-start.5
  1.6 0.7 shard_map.65
  2.3 0.0 copy-start
  2.3 37.3 %all_to_all.10 = bf16[128,8,896]{2,1,0:T(8,128)(2,1)S(1)} all-to-all(bf16[128,8,896]{2,1,0:T(8,128)(2,1)S(1)} %bitcast.22), channel_id=1, replica_groups={{0,32,64,96,8,40,72,104,16,48,80,112,24,56,88,120,2,34,66,98,10,42,74,1..., dimensions={0} | all-to-all | bytes 3670016 | tf_op jit(solution)/shard_map/all_to_all | solution.py:197
  39.6 0.0 slice-done
  39.6 0.0 slice-done.2
  39.6 0.0 slice-done.4
  39.6 0.0 slice-done.1
  39.6 0.0 slice-done.3
  39.6 0.0 slice-done.5
  39.6 0.0 copy-done
  39.6 6.4 %shard_map.66 = (bf16[1024,896]{1,0:T(8,128)(2,1)S(1)}, bf16[128,1024]{1,0:T(8,128)(2,1)S(1)}) custom-call(f32[8,16]{1,0:T(8,128)S(1)} %convert_bitcast_fusion.ids_ref, f32[8,16]{1,0:T(8,128)S(1)} %bitcast.23, bf16[64,1024]{1,0:T(8,128)(2,1)S(1)} %shard_map.64.chosen_ref, bf16[1024,896]{1,0:T(8,128)(2,1)S(1)} %bitcast.20, bf16[3584,1024]{1,0:T(8,128)(2,1)S(1)} %bitcast.13, ...), custom_call_target="tpu_custom_call" | custom-call | tf_op jit(solution)/shard_map/pallas_call | solution.py:180
  46.0 31.6 %all_to_all.11 = bf16[128,8,896]{2,1,0:T(8,128)(2,1)S(1)} all-to-all(bf16[128,8,896]{2,1,0:T(8,128)(2,1)S(1)} %bitcast.21), channel_id=1, replica_groups={{0,32,64,96,8,40,72,104,16,48,80,112,24,56,88,120,2,34,66,98,10,42,74,1..., dimensions={0} | all-to-all | bytes 3670016 | tf_op jit(solution)/shard_map/all_to_all | solution.py:197
  77.6 1.1 %shard_map.67 = bf16[16,3584]{1,0:T(8,128)(2,1)} custom-call(bf16[128,1024]{1,0:T(8,128)(2,1)S(1)} %get-tuple-element.7.weights_ref, bf16[1024,896]{1,0:T(8,128)(2,1)S(1)} %bitcast.10), custom_call_target="tpu_custom_call" | custom-call | tf_op jit(solution)/shard_map/pallas_call | solution.py:116
  (3 shorter events, 0.0 us)
Async XLA Ops:
  0.7 0.9 %copy-start.1 = (bf16[16,3584]{1,0:T(8,128)(2,1)S(1)}, bf16[16,3584]{1,0:T(8,128)(2,1)}, u32[]{:S(2)}) copy-start(bf16[16,3584]{1,0:T(8,128)(2,1)} %tokens_ref.1) | copy-start | bytes 344068
  0.7 38.9 %slice-start = ((s8[7340032]{0:T(1024)(128)(4,1)}), s8[4194304]{0:T(1024)(128)(4,1)S(1)}, s32[]{:S(2)}) async-start(s8[7340032]{0:T(1024)(128)(4,1)} %bitcast.11), calls=%async_computation.2 | async-start | bytes 8388608
  0.7 38.9 %slice-start.2 = ((s8[7340032]{0:T(1024)(128)(4,1)}), s8[4194304]{0:T(1024)(128)(4,1)S(1)}, s32[]{:S(2)}) async-start(s8[7340032]{0:T(1024)(128)(4,1)} %bitcast.14), calls=%async_computation.4 | async-start | bytes 8388608
  0.7 38.9 %slice-start.4 = ((s8[7340032]{0:T(1024)(128)(4,1)}), s8[4194304]{0:T(1024)(128)(4,1)S(1)}, s32[]{:S(2)}) async-start(s8[7340032]{0:T(1024)(128)(4,1)} %bitcast.17), calls=%async_computation.6 | async-start | bytes 8388608
  1.6 38.0 %slice-start.1 = ((s8[7340032]{0:T(1024)(128)(4,1)}), s8[3145728]{0:T(1024)(128)(4,1)S(1)}, s32[]{:S(2)}) async-start(s8[7340032]{0:T(1024)(128)(4,1)} %bitcast.11), calls=%async_computation.3 | async-start | bytes 6291456
  1.6 38.0 %slice-start.3 = ((s8[7340032]{0:T(1024)(128)(4,1)}), s8[3145728]{0:T(1024)(128)(4,1)S(1)}, s32[]{:S(2)}) async-start(s8[7340032]{0:T(1024)(128)(4,1)} %bitcast.14), calls=%async_computation.5 | async-start | bytes 6291456
  1.6 38.0 %slice-start.5 = ((s8[7340032]{0:T(1024)(128)(4,1)}), s8[3145728]{0:T(1024)(128)(4,1)S(1)}, s32[]{:S(2)}) async-start(s8[7340032]{0:T(1024)(128)(4,1)} %bitcast.17), calls=%async_computation.7 | async-start | bytes 6291456
  2.3 37.3 %copy-start = (f32[16,8]{0,1:T(8,128)S(1)}, f32[16,8]{0,1:T(8,128)}, u32[]{:S(2)}) copy-start(f32[16,8]{0,1:T(8,128)} %param.8) | copy-start | bytes 1540

commit v8 on v7

--- a/solution.py
+++ b/solution.py
@@ -9,7 +9,10 @@
 QUARTERS = 4
 PART = CAPACITY * QUARTERS
 LANES = 128
-ORDER = [x * 32 + y * 8 + z * 2 + c for c in range(2) for z in range(4) for y in range(4) for x in range(4)]
+ORDER = [
+    x * 32 + (x + y) % 4 * 8 + (x + z) % 4 * 2 + c
+    for c in range(2) for z in range(4) for y in range(4) for x in range(4)
+]
 VMEM = pl.BlockSpec(memory_space=pltpu.VMEM)
 
 
@@ -201,7 +204,8 @@
 def on_device(tokens, expert_ids, gates, w_gate, w_up, w_down):
     experts = lax.axis_size("group") * lax.axis_size("local")
     e = expert_ids
-    message = (e & 1) * 64 + ((e >> 1) & 3) * 16 + ((e >> 3) & 3) * 4 + (e >> 5)
+    x = e >> 5
+    message = (e & 1) * 64 + (((e >> 1) - x) & 3) * 16 + (((e >> 3) - x) & 3) * 4 + x
     ids = message.T.astype(jnp.float32)
     chosen = choose(ids, experts)
     got = swap(pack(chosen, tokens), experts)

time: 78.9 us -> 80.8 us (1.024)
  blocking collectives: 68.9 us -> 70.8 us
    all_to_all x2, blocking collectives: 68.9 us -> 70.8 us  [swap(): lax.all_to_all(parts, ('group', 'local'), axis_index_groups=[ORDER], spli...]
where the time goes in v8:
time: 80.8 us; the launch traced here: 80.6 us
  blocking collectives  70.8 us (88%)
  Pallas kernels  8.52 us (11%)
    all_to_all x2, blocking collectives, swap(): lax.all_to_all(parts, ('group', 'local'), axis_index_groups=[ORDER], spli...  70.8 us
    pallas_call x1, Pallas kernels, expert_ffn(): pl.pallas_call(expert_kernel, out_shape=(jax.ShapeDtypeStruct(got.shape,...  6.36 us

profile of v8, /device:TPU:1, one launch (start us, length us, event | category | flops | bytes accessed | tf_op | source)
XLA Modules:
  0.0 80.6 jit_solution(13846209999680658219)
XLA Ops:
  0.0 0.7 convert_bitcast_fusion.ids_ref
  0.7 0.0 copy-start.1
  0.7 0.0 slice-start
  0.7 0.0 slice-start.2
  0.7 0.0 slice-start.4
  0.7 0.4 shard_map.64.chosen_ref
  1.1 0.5 copy-done.1
  1.6 0.0 slice-start.1
  1.6 0.0 slice-start.3
  1.6 0.0 slice-start.5
  1.6 0.7 shard_map.65
  2.3 0.0 copy-start
  2.3 39.3 %all_to_all.10 = bf16[128,8,896]{2,1,0:T(8,128)(2,1)S(1)} all-to-all(bf16[128,8,896]{2,1,0:T(8,128)(2,1)S(1)} %bitcast.22), channel_id=1, replica_groups={{0,42,84,126,8,50,92,102,16,58,68,110,24,34,76,118,2,44,86,120,10,52,94..., dimensions={0} | all-to-all | bytes 3670016 | tf_op jit(solution)/shard_map/all_to_all | solution.py:200
  41.6 0.0 slice-done
  41.6 0.0 slice-done.2
  41.6 0.0 slice-done.4
  41.6 0.0 slice-done.1
  41.6 0.0 slice-done.3
  41.6 0.0 slice-done.5
  41.6 0.0 copy-done
  41.6 6.4 %shard_map.66 = (bf16[1024,896]{1,0:T(8,128)(2,1)S(1)}, bf16[128,1024]{1,0:T(8,128)(2,1)S(1)}) custom-call(f32[8,16]{1,0:T(8,128)S(1)} %convert_bitcast_fusion.ids_ref, f32[8,16]{1,0:T(8,128)S(1)} %bitcast.23, bf16[64,1024]{1,0:T(8,128)(2,1)S(1)} %shard_map.64.chosen_ref, bf16[1024,896]{1,0:T(8,128)(2,1)S(1)} %bitcast.20, bf16[3584,1024]{1,0:T(8,128)(2,1)S(1)} %bitcast.13, ...), custom_call_target="tpu_custom_call" | custom-call | tf_op jit(solution)/shard_map/pallas_call | solution.py:183
  48.0 31.5 %all_to_all.11 = bf16[128,8,896]{2,1,0:T(8,128)(2,1)S(1)} all-to-all(bf16[128,8,896]{2,1,0:T(8,128)(2,1)S(1)} %bitcast.21), channel_id=1, replica_groups={{0,42,84,126,8,50,92,102,16,58,68,110,24,34,76,118,2,44,86,120,10,52,94..., dimensions={0} | all-to-all | bytes 3670016 | tf_op jit(solution)/shard_map/all_to_all | solution.py:200
  79.5 1.1 %shard_map.67 = bf16[16,3584]{1,0:T(8,128)(2,1)} custom-call(bf16[128,1024]{1,0:T(8,128)(2,1)S(1)} %get-tuple-element.7.weights_ref, bf16[1024,896]{1,0:T(8,128)(2,1)S(1)} %bitcast.10), custom_call_target="tpu_custom_call" | custom-call | tf_op jit(solution)/shard_map/pallas_call | solution.py:119
  (3 shorter events, 0.0 us)
Async XLA Ops:
  0.7 0.9 %copy-start.1 = (bf16[16,3584]{1,0:T(8,128)(2,1)S(1)}, bf16[16,3584]{1,0:T(8,128)(2,1)}, u32[]{:S(2)}) copy-start(bf16[16,3584]{1,0:T(8,128)(2,1)} %tokens_ref.1) | copy-start | bytes 344068
  0.7 40.9 %slice-start = ((s8[7340032]{0:T(1024)(128)(4,1)}), s8[4194304]{0:T(1024)(128)(4,1)S(1)}, s32[]{:S(2)}) async-start(s8[7340032]{0:T(1024)(128)(4,1)} %bitcast.11), calls=%async_computation.2 | async-start | bytes 8388608
  0.7 40.9 %slice-start.2 = ((s8[7340032]{0:T(1024)(128)(4,1)}), s8[4194304]{0:T(1024)(128)(4,1)S(1)}, s32[]{:S(2)}) async-start(s8[7340032]{0:T(1024)(128)(4,1)} %bitcast.14), calls=%async_computation.4 | async-start | bytes 8388608
  0.7 40.9 %slice-start.4 = ((s8[7340032]{0:T(1024)(128)(4,1)}), s8[4194304]{0:T(1024)(128)(4,1)S(1)}, s32[]{:S(2)}) async-start(s8[7340032]{0:T(1024)(128)(4,1)} %bitcast.17), calls=%async_computation.6 | async-start | bytes 8388608
  1.6 40.0 %slice-start.1 = ((s8[7340032]{0:T(1024)(128)(4,1)}), s8[3145728]{0:T(1024)(128)(4,1)S(1)}, s32[]{:S(2)}) async-start(s8[7340032]{0:T(1024)(128)(4,1)} %bitcast.11), calls=%async_computation.3 | async-start | bytes 6291456
  1.6 40.0 %slice-start.3 = ((s8[7340032]{0:T(1024)(128)(4,1)}), s8[3145728]{0:T(1024)(128)(4,1)S(1)}, s32[]{:S(2)}) async-start(s8[7340032]{0:T(1024)(128)(4,1)} %bitcast.14), calls=%async_computation.5 | async-start | bytes 6291456
  1.6 40.0 %slice-start.5 = ((s8[7340032]{0:T(1024)(128)(4,1)}), s8[3145728]{0:T(1024)(128)(4,1)S(1)}, s32[]{:S(2)}) async-start(s8[7340032]{0:T(1024)(128)(4,1)} %bitcast.17), calls=%async_computation.7 | async-start | bytes 6291456
  2.3 39.3 %copy-start = (f32[16,8]{0,1:T(8,128)S(1)}, f32[16,8]{0,1:T(8,128)}, u32[]{:S(2)}) copy-start(f32[16,8]{0,1:T(8,128)} %param.8) | copy-start | bytes 1540
